TPU v7x, 256 devices: a whole 4x4x8 slice. The times are simulated.
256 devices in a mesh: aux: 16 (over x, y), orb: 16 (over z, core).
Axes of the slice: x: 4, y: 4, z: 8, core: 2. Of those that a mesh axis runs over, the one named last changes fastest.
Arguments:
- integrals: bfloat16 [32, 15360, 2048], P(None, 'aux', 'orb'), may hold values from -6 to 6
- coeffs: bfloat16 [2048, 2048], P('orb'), may hold values from -1 to 1
- domains: int32 [32], replicated, may hold values from 0 to 15
- eps_occ: float32 [32], replicated, may hold values from -1.5 to -0.3
- eps_vir: float32 [2048], replicated, may hold values from 0.1 to 2.5
- pair_mask: int32 [32, 32], P('aux', 'orb'), may hold values 0 or 1
Outputs:
- amplitudes: bfloat16 [32, 128, 32, 128], P('aux', None, 'orb')
- energies: float32 [32, 32], P('aux', 'orb')
Inputs may be any that keep to these rules, and one draw needn't show every extreme that they name: `domains`: each entry names one of the 16 virtual blocks.
All inputs are finite; a program needn't handle non-finite values. No bound on the sum of `pair_mask` on one device may be relied on, other than what follows from the above.
Results may differ from a plain program's by a relative error of at most 0.019.
Values may be sent and summed in bfloat16 or wider, within the bound.
No kernel may reach another device: no remote copies, remote signals or barrier semaphores. Data moves between devices by JAX's collectives and lax.ppermute only.
A program may use at most 64 MiB of HBM per device.

v0:
```python
import jax
import jax.numpy as jnp
from jax import lax
from jax.sharding import PartitionSpec as P

NAUX = 15360
BS = 128


def shards(integrals, coeffs, domains, eps_occ, eps_vir, pair_mask):
    occupied, aux_rows, ao_local = integrals.shape
    vir_blocks = coeffs.shape[1] // BS
    selector = domains[:, None] == jnp.arange(vir_blocks, dtype=jnp.int32)[None, :]
    chosen = jnp.einsum(
        "in,mnb->imb",
        selector.astype(jnp.bfloat16),
        coeffs.reshape(ao_local, vir_blocks, BS),
        preferred_element_type=jnp.float32,
    ).astype(jnp.bfloat16)
    orb_index = lax.axis_index("orb")
    own_count = occupied // lax.axis_size("orb")
    own_blocks = lax.psum_scatter(
        jnp.einsum("ipm,imb->ipb", integrals, chosen, preferred_element_type=jnp.float32).astype(
            jnp.bfloat16
        ),
        "orb",
        scatter_dimension=0,
        tiled=True,
    )
    all_blocks = lax.all_gather(own_blocks, "orb", axis=0, tiled=True)
    aux_index = lax.axis_index("aux")
    row_count = occupied // lax.axis_size("aux")
    totals = lax.psum_scatter(
        jnp.einsum(
            "jpb,ipa->jbia", all_blocks, own_blocks, preferred_element_type=jnp.float32
        ).astype(jnp.bfloat16),
        "aux",
        scatter_dimension=0,
        tiled=True,
    ).astype(jnp.float32)
    pair_ints = totals * (1.0 / jnp.sqrt(jnp.float32(NAUX)))
    vir_energy = jnp.dot(
        selector.astype(jnp.float32),
        eps_vir.reshape(vir_blocks, BS),
        precision=lax.Precision.HIGHEST,
    )
    vir_rows = lax.dynamic_slice_in_dim(vir_energy, aux_index * row_count, row_count, 0)
    vir_cols = lax.dynamic_slice_in_dim(vir_energy, orb_index * own_count, own_count, 0)
    occ_rows = lax.dynamic_slice_in_dim(eps_occ, aux_index * row_count, row_count, 0)
    occ_cols = lax.dynamic_slice_in_dim(eps_occ, orb_index * own_count, own_count, 0)
    denominator = (
        vir_rows[:, :, None, None]
        + vir_cols[None, None, :, :]
        - occ_rows[:, None, None, None]
        - occ_cols[None, None, :, None]
    )
    screen = pair_mask.astype(jnp.float32)
    amplitudes = screen[:, None, :, None] * pair_ints / denominator
    energies = -jnp.sum(pair_ints * amplitudes, axis=(1, 3)) / float(BS * BS)
    return (amplitudes.astype(jnp.bfloat16), energies)


def solution(mesh):
    return jax.shard_map(
        shards,
        mesh=mesh,
        in_specs=(P(None, "aux", "orb"), P("orb", None), P(), P(), P(), P("aux", "orb")),
        out_specs=(P("aux", None, "orb", None), P("aux", "orb")),
        check_vma=False,
    )
```

profile of v0, /device:TPU:96, one launch (start us, length us, event | category | flops | bytes accessed | tf_op | source)
XLA Modules:
  0.0 237.9 jit_solution(13202559230321626064)
XLA Ops:
  7.2 0.0 copy-start
  7.2 0.0 reduce-scatter.3.cloned.1.call-start
  7.2 1.1 copy.12
  8.4 1.1 fusion.12
  9.5 8.5 %convert_bitcast_fusion = bf16[32,960,128]{2,1,0:T(8,128)(2,1)} fusion(bf16[32,960,128]{2,1,0:T(8,128)(2,1)} %param.6, bf16[32,128,128]{2,0,1:T(8,128)(2,1)S(1)} %fusion.12), kind=kOutput, calls=%fused_computation.2 | convolution fusion | flops 1010565120 | bytes 16777216 | tf_op jit(solution)/shard_map/ipm,imb->ipb/dot_general | solution.py:23
  18.0 0.0 reduce-scatter.3.cloned.1.call-update
  18.1 0.0 all-gather.2.cloned.1.call-start
  18.1 67.5 %reduce-scatter.3.cloned.1.call-done = bf16[2,960,128]{2,1,0:T(8,128)(2,1)} async-done(((bf16[32,960,128]{2,1,0:T(8,128)(2,1)}), bf16[2,960,128]{2,1,0:T(8,128)(2,1)}) %reduce-scatter.3.cloned.1.call-update) | async-done | bytes 491536 | tf_op jit(solution)/shard_map/reduce_scatter | solution.py:22
  85.6 0.0 all-gather.2.cloned.1.call-update
  85.7 0.0 copy-start.1
  85.7 0.0 copy-start.3
  85.7 0.0 copy-start.2
  85.7 0.0 reduce-scatter.5.cloned.1.call-start
  85.7 57.2 %all-gather.2.cloned.1.call-done = bf16[32,960,128]{2,1,0:T(8,128)(2,1)} async-done(((bf16[2,960,128]{2,1,0:T(8,128)(2,1)}), bf16[32,960,128]{2,1,0:T(8,128)(2,1)}) %all-gather.2.cloned.1.call-update) | async-done | bytes 7864336 | tf_op jit(solution)/shard_map/all_gather | solution.py:30
  142.9 7.1 %fusion.2 = bf16[32,128,2,128]{3,1,2,0:T(8,128)(2,1)} fusion(bf16[32,960,128]{2,1,0:T(8,128)(2,1)} %all-gather.2.cloned.1.call-done, bf16[2,960,128]{2,1,0:T(8,128)(2,1)} %reduce-scatter.3.cloned.1.call-done), kind=kOutput, calls=%fused_computation.4 | convolution fusion | flops 2014314496 | bytes 10452992 | tf_op jit(solution)/shard_map/jpb,ipa->jbia/dot_general | solution.py:34
  150.1 0.0 reduce-scatter.5.cloned.1.call-update
  150.1 0.0 copy-done.1
  150.1 0.1 fusion.17
  150.2 0.0 copy-done
  150.2 0.0 copy-done.3
  150.2 0.2 fusion.10
  150.4 0.0 copy-done.2
  150.4 78.4 %reduce-scatter.5.cloned.1.call-done = bf16[2,128,2,128]{3,1,2,0:T(8,128)(2,1)} async-done(((bf16[32,128,2,128]{3,1,2,0:T(8,128)(2,1)}), bf16[2,128,2,128]{3,1,2,0:T(8,128)(2,1)}) %reduce-scatter.5.cloned.1.call-update) | async-done | bytes 131088 | tf_op jit(solution)/shard_map/reduce_scatter | solution.py:33
  228.9 1.2 fusion.8
  230.0 0.8 copy.9
  230.8 0.6 negate_multiply_fusion
  (2 shorter events, 0.0 us)
Async XLA Ops:
  7.2 143.0 %copy-start = (f32[2048]{0:T(1024)S(1)}, f32[2048]{0:T(1024)}, u32[]{:S(2)}) copy-start(f32[2048]{0:T(1024)} %param.10) | copy-start | bytes 24580
  7.2 78.5 %reduce-scatter.3.cloned.1.call-start = ((), (), s32[]{:S(2)}) async-start(), calls=%async_computation.2 | async-start | bytes 8355840 | tf_op jit(solution)/shard_map/reduce_scatter | solution.py:22
  18.1 124.9 %all-gather.2.cloned.1.call-start = ((), (), s32[]{:S(2)}) async-start(), calls=%async_computation.3 | async-start | bytes 8355840 | tf_op jit(solution)/shard_map/all_gather | solution.py:30
  85.7 64.4 %copy-start.1 = (f32[32]{0:T(128)S(1)}, f32[32]{0:T(128)}, u32[]{:S(2)}) copy-start(f32[32]{0:T(128)} %param.9) | copy-start | bytes 388
  85.7 64.5 %copy-start.3 = (s32[32]{0:T(128)S(1)}, s32[32]{0:T(128)}, u32[]{:S(2)}) copy-start(s32[32]{0:T(128)} %param.8) | copy-start | bytes 388
  85.7 64.7 %copy-start.2 = (s32[2,2]{1,0:T(2,128)S(1)}, s32[2,2]{1,0:T(2,128)}, u32[]{:S(2)}) copy-start(s32[2,2]{1,0:T(2,128)} %param.11) | copy-start | bytes 52
  85.7 143.2 %reduce-scatter.5.cloned.1.call-start = ((), (), s32[]{:S(2)}) async-start(), calls=%async_computation.4 | async-start | bytes 2228224 | tf_op jit(solution)/shard_map/reduce_scatter | solution.py:33
Sparse Core Ops, SparseCore 0:
  18.2 67.3 reduce-scatter.2
  87.5 55.4 all-gather.1
  150.2 78.6 reduce-scatter.4
where the time goes:
time: 239 us; the launch traced here: 238 us
  waiting for transfers between devices  203 us (85%)
  matrix products  16.9 us (7%)
  between operations  13.8 us (6%)
    reduce_scatter x1, waiting for transfers between devices, shards(): lax.psum_scatter(jnp.einsum('jpb,ipa->jbia', all_blocks, own_blocks, pref...  78.4 us
    reduce_scatter x1, waiting for transfers between devices, shards(): lax.psum_scatter(jnp.einsum('ipm,imb->ipb', integrals, chosen, preferred_...  67.5 us
    all_gather x1, waiting for transfers between devices, shards(): all_blocks = lax.all_gather(own_blocks, 'orb', axis=0, tiled=True)  57.2 us
    dot_general x1, matrix products, shards(): jnp.einsum('ipm,imb->ipb', integrals, chosen, preferred_element_type=jnp....  8.52 us
    dot_general x1, matrix products, shards(): jnp.einsum('jpb,ipa->jbia', all_blocks, own_blocks, preferred_element_typ...  7.11 us
  transfers between devices with their start and end apart: 3, of which 3 were waited for; matrix products, arithmetic and copies ran while one was open for 0% of the time, Pallas kernels for 0%

commit v1 on v0

v1 whole, which is shorter than its diff:
```python
import jax
import jax.numpy as jnp
import numpy as np
from jax import lax
from jax.experimental import pallas as pl
from jax.experimental.pallas import tpu as pltpu
from jax.sharding import PartitionSpec as P

NAUX = 15360
BS = 128
CHIPS = 8
OWN = 4
EXTRA = 16
ROWS = 2 * BS + EXTRA
EARLY = 10
SLOTS = 16


def transform_kernel(meta, a_ref, c0, c1, c2, c3, out_ref):
    for q, c in enumerate((c0, c1, c2, c3)):
        out_ref[0, :, q * BS : (q + 1) * BS] = jnp.dot(
            a_ref[q], c[...], preferred_element_type=jnp.float32
        ).astype(jnp.bfloat16)


def combine_kernel(meta, a_ref, c0, c1, c2, c3, y_ref, out_ref):
    for q, c in enumerate((c0, c1, c2, c3)):
        lanes = slice(q * BS, (q + 1) * BS)
        total = jnp.dot(a_ref[q], c[...], preferred_element_type=jnp.float32)
        out_ref[0, :, lanes] = (total + y_ref[0, :, lanes].astype(jnp.float32)).astype(jnp.bfloat16)


def combine_split_kernel(meta, a_ref, c0, c1, c2, c3, y_ref, up_ref, down_ref):
    rows = up_ref.shape[0]
    for q, c in enumerate((c0, c1, c2, c3)):
        lanes = slice(q * BS, (q + 1) * BS)
        total = jnp.dot(a_ref[q], c[...], preferred_element_type=jnp.float32)
        total = (total + y_ref[0, :, lanes].astype(jnp.float32)).astype(jnp.bfloat16)
        up_ref[:, lanes] = total[:rows]
        down_ref[:, lanes] = total[rows:]


def chunk_call(meta, integrals, coeffs, first, count, other, received=None, split=False):
    half = integrals.shape[1] // 2
    width = OWN * BS

    def a_map(n, m):
        return (m[1 + first + n], (1 - m[0]) if other else m[0], 0)

    def c_map(q):
        return lambda n, m: (0, m[1 + CHIPS + OWN * m[1 + first + n] + q])

    in_specs = [pl.BlockSpec((OWN, half, BS), a_map)]
    in_specs += [pl.BlockSpec((BS, BS), c_map(q)) for q in range(OWN)]
    operands = [integrals] + [coeffs] * OWN
    block = pl.BlockSpec((1, half, width), lambda n, m: (n, 0, 0))
    if received is not None:
        in_specs.append(block)
        operands.append(received)
    if split:
        body = combine_split_kernel
        part = pl.BlockSpec((half // 2, width), lambda n, m: (0, 0))
        out_specs = (part, part)
        out_shape = (jax.ShapeDtypeStruct((half // 2, width), jnp.bfloat16),) * 2
    else:
        body = transform_kernel if received is None else combine_kernel
        out_specs = block
        out_shape = jax.ShapeDtypeStruct((count, half, width), jnp.bfloat16)
    return pl.pallas_call(
        body,
        grid_spec=pltpu.PrefetchScalarGridSpec(
            num_scalar_prefetch=1, grid=(count,), in_specs=in_specs, out_specs=out_specs
        ),
        out_shape=out_shape,
        compiler_params=pltpu.CompilerParams(vmem_limit_bytes=32 * 2**20),
    )(meta, *operands)


def gram(left, right):
    return lax.dot_general(
        left, right, (((0,), (0,)), ((), ())), preferred_element_type=jnp.float32
    )


def orbital(ref, index):
    return ref[:, pl.ds(pl.multiple_of(index * BS, BS), BS)]


def put(out_ref, slot, product, received):
    for m in range(2):
        value = product[:, m * BS : (m + 1) * BS]
        if received is not None:
            value = value + received[slot, m * BS : (m + 1) * BS].astype(jnp.float32)
        out_ref[slot, m * BS : (m + 1) * BS] = value.astype(jnp.bfloat16)
    out_ref[slot, 2 * BS :] = jnp.zeros((EXTRA, BS), jnp.bfloat16)


def block_products(h, left_ref, right_ref, slot, out_ref, received):
    left = jnp.concatenate([orbital(left_ref, h), orbital(left_ref, 2 + h)], axis=1)
    product = gram(left, right_ref[...])
    for l in range(2):
        for m in range(2):
            piece = product[l * BS : (l + 1) * BS, 2 * m * BS : 2 * (m + 1) * BS]
            put(out_ref, slot + 2 * l + m, piece, received)


def early_kernel(other, meta, own_ref, prev_ref, next_ref, *refs):
    received, out_ref = refs if len(refs) == 2 else (None, refs[0])
    h = (1 - meta[0]) if other else meta[0]
    block_products(h, own_ref, next_ref, 0, out_ref, received)
    block_products(h, prev_ref, next_ref, 4, out_ref, received)
    put(out_ref, 8, gram(orbital(own_ref, h), own_ref[:, 2 * BS :]), received)
    pair = jnp.concatenate([orbital(own_ref, 2 * h), orbital(own_ref, 2 * h + 1)], axis=1)
    diag = gram(pair, pair)
    row = lax.broadcasted_iota(jnp.int32, (BS, BS), 0)
    col = lax.broadcasted_iota(jnp.int32, (BS, BS), 1)
    second = diag[BS:, BS:]
    packed = jnp.where(row >= col, diag[:BS, :BS], second)
    line = jnp.sum(jnp.where(row == col, second, 0.0), axis=0, keepdims=True)
    line = jnp.broadcast_to(line, (EXTRA, BS))
    cross = diag[:BS, BS:]
    if received is not None:
        packed = packed + received[9, :BS].astype(jnp.float32)
        cross = cross + received[9, BS : 2 * BS].astype(jnp.float32)
        line = line + received[9, 2 * BS :].astype(jnp.float32)
    out_ref[9, :BS] = packed.astype(jnp.bfloat16)
    out_ref[9, BS : 2 * BS] = cross.astype(jnp.bfloat16)
    out_ref[9, 2 * BS :] = line.astype(jnp.bfloat16)


def late_products(h, chip, prev_ref, next2_ref, prev2_ref, slot, out_ref, received):
    block_products(h, prev_ref, next2_ref, slot, out_ref, received)

    def opposite(left, right):
        product = gram(left, right[...])
        for m in range(2):
            put(out_ref, slot + 4 + m, product[:, 2 * m * BS : 2 * (m + 1) * BS], received)

    @pl.when(chip < CHIPS // 2)
    def _():
        opposite(orbital(prev2_ref, h), next2_ref)

    @pl.when(chip >= CHIPS // 2)
    def _():
        opposite(orbital(next2_ref, 2 + h), prev2_ref)


def late_send_kernel(meta, prev_ref, next2_ref, prev2_ref, out_ref):
    late_products(1 - meta[0], meta[1], prev_ref, next2_ref, prev2_ref, 0, out_ref, None)


class Shifted:
    def __init__(self, ref, by):
        self.ref, self.by = ref, by

    def __getitem__(self, key):
        return self.ref[(key[0] - self.by,) + key[1:]]


def late_own_kernel(meta, prev_ref, next2_ref, prev2_ref, early_ref, received, out_ref):
    out_ref[:EARLY] = early_ref[...]
    late_products(
        meta[0], meta[1], prev_ref, next2_ref, prev2_ref, EARLY, out_ref, Shifted(received, EARLY)
    )


def pair_call(body, meta, operands, slots):
    return pl.pallas_call(
        body,
        grid_spec=pltpu.PrefetchScalarGridSpec(
            num_scalar_prefetch=1,
            grid=(1,),
            in_specs=[
                pl.BlockSpec(x.shape, lambda n, m, nd=x.ndim: (0,) * nd) for x in operands
            ],
            out_specs=pl.BlockSpec((slots, ROWS, BS), lambda n, m: (0, 0, 0)),
        ),
        out_shape=jax.ShapeDtypeStruct((slots, ROWS, BS), jnp.bfloat16),
        compiler_params=pltpu.CompilerParams(vmem_limit_bytes=32 * 2**20),
    )(meta, *operands)


def final_kernel(meta, eps_occ, mask, first_ref, second_ref, vir_ref, amp_ref, energy_ref, t_ref):
    kind = meta[0]
    units = [slice(0, BS), slice(BS, 2 * BS)]

    @pl.when(kind == 0)
    def _():
        for j, ref in enumerate((first_ref, second_ref)):
            for i in range(2):
                t_ref[j, i] = ref[units[i]].astype(jnp.float32)

    @pl.when(kind == 1)
    def _():
        for i, ref in enumerate((second_ref, first_ref)):
            for j in range(2):
                t_ref[j, i] = ref[units[j]].astype(jnp.float32).T

    @pl.when(kind == 2)
    def _():
        row = lax.broadcasted_iota(jnp.int32, (BS, BS), 0)
        col = lax.broadcasted_iota(jnp.int32, (BS, BS), 1)
        packed = first_ref[units[0]].astype(jnp.float32)
        flipped = packed.T
        line = first_ref[2 * BS : 2 * BS + EXTRA].astype(jnp.float32)[:1]
        t_ref[0, 0] = jnp.where(row >= col, packed, flipped)
        t_ref[1, 1] = jnp.where(row < col, packed, jnp.where(row > col, flipped, line))
        cross = first_ref[units[1]].astype(jnp.float32)
        t_ref[0, 1] = cross
        t_ref[1, 0] = cross.T

    scale = 1.0 / np.sqrt(np.float32(NAUX))
    for j in range(2):
        jj = 2 * meta[1] + j
        vir_j = vir_ref[pl.ds(meta[3 + jj], 1), :]
        rows = jnp.broadcast_to(vir_j, (BS, BS)).T
        for i in range(2):
            ii = 2 * meta[2] + i
            vir_i = vir_ref[pl.ds(meta[3 + ii], 1), :]
            denominator = rows + vir_i - eps_occ[jj] - eps_occ[ii]
            pair = t_ref[j, i] * scale
            keep = mask[j, i].astype(jnp.float32)
            amp = keep * pair / denominator
            amp_ref[j, :, i * BS : (i + 1) * BS] = amp.astype(jnp.bfloat16)
            energy = jnp.sum(jnp.sum(pair * amp, axis=1, keepdims=True), axis=0, keepdims=True)
            energy_ref[2 * j + i : 2 * j + i + 1] = jnp.broadcast_to(
                energy * (-1.0 / (BS * BS)), (1, BS)
            )


def final_call(meta, eps_occ, mask, first, second, vir):
    return pl.pallas_call(
        final_kernel,
        grid_spec=pltpu.PrefetchScalarGridSpec(
            num_scalar_prefetch=3,
            grid=(1,),
            in_specs=[
                pl.BlockSpec(first.shape, lambda n, *m: (0, 0)),
                pl.BlockSpec(second.shape, lambda n, *m: (0, 0)),
                pl.BlockSpec(vir.shape, lambda n, *m: (0, 0)),
            ],
            out_specs=(
                pl.BlockSpec((2, BS, 2 * BS), lambda n, *m: (0, 0, 0)),
                pl.BlockSpec((8, BS), lambda n, *m: (0, 0)),
            ),
            scratch_shapes=[pltpu.VMEM((2, 2, BS, BS), jnp.float32)],
        ),
        out_shape=(
            jax.ShapeDtypeStruct((2, BS, 2 * BS), jnp.bfloat16),
            jax.ShapeDtypeStruct((8, BS), jnp.float32),
        ),
    )(meta, eps_occ, mask, first, second, vir)


def slot_pairs(chip):
    sup = lambda off, l: 2 * ((chip + off) % CHIPS) + l
    pairs = [(sup(0, l), sup(1, m)) for l in range(2) for m in range(2)]
    pairs += [(sup(-1, l), sup(1, m)) for l in range(2) for m in range(2)]
    pairs += [(sup(0, 0), sup(0, 1)), None]
    pairs += [(sup(-1, l), sup(2, m)) for l in range(2) for m in range(2)]
    if chip < CHIPS // 2:
        pairs += [(sup(-2, 0), sup(2, m)) for m in range(2)]
    else:
        pairs += [(sup(2, 1), sup(-2, m)) for m in range(2)]
    return pairs


def delivery():
    rounds = ([], [])
    kind = np.full((SLOTS, SLOTS), -1, np.int32)
    for chip in range(CHIPS):
        for slot, pair in enumerate(slot_pairs(chip)):
            source = [slot * SLOTS + 2 * chip + core for core in range(2)]
            if pair is None:
                for core in range(2):
                    o = 2 * chip + core
                    rounds[0].append((source[core], o * SLOTS + o))
                    kind[o, o] = 2
                continue
            u, v = pair
            owners = [u * SLOTS + v, v * SLOTS + u]
            kind[u, v], kind[v, u] = 0, 1
            rounds[0].extend([(source[0], owners[0]), (source[1], owners[1])])
            rounds[1].extend([(source[0], owners[1]), (source[1], owners[0])])
    assert (kind >= 0).all()
    return rounds, kind


def shards(integrals, coeffs, domains, eps_occ, eps_vir, pair_mask):
    aux = lax.axis_index("aux")
    orb = lax.axis_index("orb")
    chip = orb // 2
    core = orb % 2
    half = integrals.shape[1] // 2
    quarter = half // 2

    n_orb = 2 * CHIPS
    swap = lambda x: lax.ppermute(x, "orb", [(o, o ^ 1) for o in range(n_orb)])
    up = lambda x: lax.ppermute(x, "orb", [(o, (o + 2) % n_orb) for o in range(n_orb)])
    down = lambda x: lax.ppermute(x, "orb", [(o, (o - 2) % n_orb) for o in range(n_orb)])

    order = jnp.array([4, 3, 5, 2, 6, 1, 7, 0], jnp.int32)
    meta = jnp.concatenate([core[None], (order + chip) % CHIPS, domains]).astype(jnp.int32)

    def combined(first, count, split=False):
        send = chunk_call(meta, integrals, coeffs, first, count, True)
        return chunk_call(meta, integrals, coeffs, first, count, False, swap(send), split)

    start_up, start_down = combined(0, 1, True)
    x1 = combined(1, 2)
    x2 = combined(3, 5)
    up_sum, down_sum = up(start_up), down(start_down)
    up_sum = jnp.concatenate([x1[0, :quarter] + up_sum, x1[0, quarter:]], axis=0)
    down_sum = jnp.concatenate([x1[1, :quarter], x1[1, quarter:] + down_sum], axis=0)
    for step in range(2):
        up_sum, down_sum = up(up_sum), down(down_sum)
        up_sum = x2[2 * step] + up_sum
        down_sum = x2[2 * step + 1] + down_sum
    up_sum, down_sum = up(up_sum), down(down_sum)
    f32 = jnp.float32
    own = (x2[4].astype(f32) + up_sum.astype(f32) + down_sum.astype(f32)).astype(jnp.bfloat16)

    prev, next_ = up(own), down(own)
    prev2, next2 = up(prev), down(next_)

    where = jnp.stack([core, chip]).astype(jnp.int32)
    send = pair_call(lambda *r: early_kernel(True, *r), where, (own, prev, next_), EARLY)
    early = pair_call(
        lambda *r: early_kernel(False, *r), where, (own, prev, next_, swap(send)), EARLY
    )
    send = pair_call(late_send_kernel, where, (prev, next2, prev2), SLOTS - EARLY)
    sums = pair_call(
        late_own_kernel, where, (prev, next2, prev2, early, swap(send)), SLOTS
    )
    parts = lax.all_to_all(sums, "aux", 0, 0, tiled=True)
    held = jnp.sum(parts.astype(f32), axis=0).astype(jnp.bfloat16)

    rounds, kind = delivery()
    first = lax.ppermute(held, ("aux", "orb"), rounds[0])
    second = lax.ppermute(held, ("aux", "orb"), rounds[1])
    info = jnp.stack([jnp.asarray(kind)[aux, orb], aux, orb]).astype(jnp.int32)
    amplitudes, energies = final_call(
        jnp.concatenate([info, domains]),
        eps_occ,
        pair_mask,
        first,
        second,
        eps_vir.reshape(-1, BS),
    )
    return amplitudes.reshape(2, BS, 2, BS), energies[:4, 0].reshape(2, 2)


def solution(mesh):
    return jax.shard_map(
        shards,
        mesh=mesh,
        in_specs=(P(None, "aux", "orb"), P("orb", None), P(), P(), P(), P("aux", "orb")),
        out_specs=(P("aux", None, "orb", None), P("aux", "orb")),
        check_vma=False,
    )
```

time: 239 us -> 154 us (0.64)
  waiting for transfers between devices: 203 us -> 88.2 us
  starting transfers between devices: 0.12 us -> 32.7 us
  Pallas kernels: 0 us -> 18.1 us
  matrix products: 16.9 us -> 0 us
  between operations: 13.8 us -> 0.88 us
  local copies, waits for them, and re-layouts: 2.07 us -> 9.24 us
    reduce_scatter x2 -> x0, waiting for transfers between devices: 146 us -> none  [the longest x1 78.4 us: shards(): lax.psum_scatter(jnp.einsum('jpb,ipa->jbia', all_blocks, own_blocks, pref...]
    ppermute x0 -> x19, waiting for transfers between devices: none -> 70.6 us  [the longest x6 36.9 us: shards(): lax.ppermute(x, 'orb', [(o, (o - 2) % n_orb) for o in range(n_orb)])]
    all_gather x1 -> x0, waiting for transfers between devices: 57.2 us -> none  [shards(): all_blocks = lax.all_gather(own_blocks, 'orb', axis=0, tiled=True)]
    ppermute x0 -> x19, starting transfers between devices: none -> 25.5 us  [the longest x6 15.4 us: shards(): lax.ppermute(x, 'orb', [(o, (o + 2) % n_orb) for o in range(n_orb)])]
    pallas_call x0 -> x11, Pallas kernels: none -> 18.1 us  [the longest x6 10 us: chunk_call(): pl.pallas_call(body, grid_spec=pltpu.PrefetchScalarGridSpec(num_scalar_pr...]
    all_to_all x0 -> x1, waiting for transfers between devices: none -> 17.6 us  [shards(): parts = lax.all_to_all(sums, 'aux', 0, 0, tiled=True)]
    dot_general x4 -> x0, matrix products: 16.9 us -> none  [the longest x1 8.52 us: shards(): jnp.einsum('ipm,imb->ipb', integrals, chosen, preferred_element_type=jnp....]
    all_to_all x0 -> x1, starting transfers between devices: none -> 7.15 us  [shards(): parts = lax.all_to_all(sums, 'aux', 0, 0, tiled=True)]
  transfers between devices with their start and end apart: 3 -> 20, of which waited for: 3 -> 13; matrix products, arithmetic and copies ran while one was open for 0% -> 2% of each run, Pallas kernels for 0% -> 7%
where the time goes in v1:
time: 154 us; the launch traced here: 152 us
  waiting for transfers between devices  88.2 us (57%)
  starting transfers between devices  32.7 us (21%)
  Pallas kernels  18.1 us (12%)
  local copies, waits for them, and re-layouts  9.24 us (6%)
  other arithmetic  3.32 us (2%)
    ppermute x6, waiting for transfers between devices, shards(): lax.ppermute(x, 'orb', [(o, (o - 2) % n_orb) for o in range(n_orb)])  36.9 us
    ppermute x6, waiting for transfers between devices, shards(): lax.ppermute(x, 'orb', [(o, (o + 2) % n_orb) for o in range(n_orb)])  20.6 us
    all_to_all x1, waiting for transfers between devices, shards(): parts = lax.all_to_all(sums, 'aux', 0, 0, tiled=True)  17.6 us
    ppermute x6, starting transfers between devices, shards(): lax.ppermute(x, 'orb', [(o, (o + 2) % n_orb) for o in range(n_orb)])  15.4 us
    pallas_call x6, Pallas kernels, chunk_call(): pl.pallas_call(body, grid_spec=pltpu.PrefetchScalarGridSpec(num_scalar_pr...  10 us
    all_to_all x1, starting transfers between devices, shards(): parts = lax.all_to_all(sums, 'aux', 0, 0, tiled=True)  7.15 us
    pallas_call x4, Pallas kernels, pair_call(): pl.pallas_call(body, grid_spec=pltpu.PrefetchScalarGridSpec(num_scalar_pr...  5.54 us
    ppermute x1, starting transfers between devices, shards(): first = lax.ppermute(held, ('aux', 'orb'), rounds[0])  5.23 us
  transfers between devices with their start and end apart: 20, of which 13 were waited for; matrix products, arithmetic and copies ran while one was open for 2% of the time, Pallas kernels for 7%

profile of v1, /device:TPU:96, one launch (start us, length us, event | category | flops | bytes accessed | tf_op | source)
XLA Modules:
  0.0 152.4 jit_solution(16448832935127349592)
XLA Ops:
  3.1 3.2 %copy-done.1 = bf16[32,960,128]{2,1,0:T(8,128)(2,1)S(1)} copy-done((bf16[32,960,128]{2,1,0:T(8,128)(2,1)S(1)}, bf16[32,960,128]{2,1,0:T(8,128)(2,1)}, u32[]{:S(2)}) %copy-start.1) | copy-done | bytes 7864344
  6.3 2.7 %shard_map.95 = bf16[5,480,512]{2,1,0:T(8,128)(2,1)S(1)} custom-call(s32[41]{0:T(128)S(1)} %pad_add_fusion.2.meta, bf16[32,960,128]{2,1,0:T(8,128)(2,1)S(1)} %copy-done.1, bf16[128,2048]{1,0:T(8,128)(2,1)S(1)} %copy-done, bf16[128,2048]{1,0:T(8,128)(2,1)S(1)} %copy-done, bf16[128,2048]{1,0:T(8,128)(2,1)S(1)} %copy-done, bf16[128,2048]{1,0:T(8,128)(2,1)S(1)} %copy-done), custom_call_target="tpu_custom_call" | custom-call | tf_op jit(solution)/shard_map/pallas_call | solution.py:69
  9.1 1.5 shard_map.97
  12.2 3.7 %collective-permute-done.2.y_ref = bf16[1,480,512]{2,1,0:T(8,128)(2,1)S(1)} collective-permute-done((bf16[1,480,512]{2,1,0:T(8,128)(2,1)S(1)}, bf16[1,480,512]{2,1,0:T(8,128)(2,1)S(1)}, u32[]{:S(2)}, u32[]{:S(2)}) %collective-permute-start.2) | collective-permute-done | bytes 491552 | tf_op jit(solution)/shard_map/ppermute | solution.py:298
  16.8 3.2 %collective-permute-start.3 = (bf16[240,512]{1,0:T(8,128)(2,1)S(1)}, bf16[240,512]{1,0:T(8,128)(2,1)S(1)}, u32[]{:S(2)}, u32[]{:S(2)}) collective-permute-start(bf16[240,512]{1,0:T(8,128)(2,1)S(1)} %get-tuple-element.6), channel_id=1, source_target_pairs={{0,2},{1,3},{2,4},{3,5},{4,6},{5,7},{6,8},{7,9},{8,10},{9,11},{10,... | collective-permute-start | bytes 737288 | tf_op jit(solution)/shard_map/ppermute | solution.py:299
  20.0 1.5 shard_map.98
  21.5 4.0 %collective-permute-done.3 = bf16[240,512]{1,0:T(8,128)(2,1)S(1)} collective-permute-done((bf16[240,512]{1,0:T(8,128)(2,1)S(1)}, bf16[240,512]{1,0:T(8,128)(2,1)S(1)}, u32[]{:S(2)}, u32[]{:S(2)}) %collective-permute-start.3) | collective-permute-done | bytes 245792 | tf_op jit(solution)/shard_map/ppermute | solution.py:299
  25.5 3.4 %collective-permute-done.7 = bf16[240,512]{1,0:T(8,128)(2,1)S(1)} collective-permute-done((bf16[240,512]{1,0:T(8,128)(2,1)S(1)}, bf16[240,512]{1,0:T(8,128)(2,1)S(1)}, u32[]{:S(2)}, u32[]{:S(2)}) %collective-permute-start.7) | collective-permute-done | bytes 245792 | tf_op jit(solution)/shard_map/ppermute | solution.py:300
  29.4 1.8 %collective-permute-start.8 = (bf16[480,512]{1,0:T(8,128)(2,1)S(1)}, bf16[480,512]{1,0:T(8,128)(2,1)S(1)}, u32[]{:S(2)}, u32[]{:S(2)}) collective-permute-start(bf16[480,512]{1,0:T(8,128)(2,1)S(1)} %pad_maximum_fusion.1), channel_id=1, source_target_pairs={{0,14},{1,15},{2,0},{3,1},{4,2},{5,3},{6,4},{7,5},{8,6},{9,7},{10,... | collective-permute-start | bytes 1474568 | tf_op jit(solution)/shard_map/ppermute | solution.py:300
  31.3 2.7 %shard_map.96 = bf16[5,480,512]{2,1,0:T(8,128)(2,1)S(1)} custom-call(s32[41]{0:T(128)S(1)} %pad_add_fusion.2.meta, bf16[32,960,128]{2,1,0:T(8,128)(2,1)S(1)} %copy-done.1, bf16[128,2048]{1,0:T(8,128)(2,1)S(1)} %copy-done, bf16[128,2048]{1,0:T(8,128)(2,1)S(1)} %copy-done, bf16[128,2048]{1,0:T(8,128)(2,1)S(1)} %copy-done, bf16[128,2048]{1,0:T(8,128)(2,1)S(1)} %copy-done, ...), custom_call_target="tpu_custom_call" | custom-call | tf_op jit(solution)/shard_map/pallas_call | solution.py:69
  34.0 7.3 %collective-permute-done.4 = bf16[480,512]{1,0:T(8,128)(2,1)S(1)} collective-permute-done((bf16[480,512]{1,0:T(8,128)(2,1)S(1)}, bf16[480,512]{1,0:T(8,128)(2,1)S(1)}, u32[]{:S(2)}, u32[]{:S(2)}) %collective-permute-start.4) | collective-permute-done | bytes 491552 | tf_op jit(solution)/shard_map/ppermute | solution.py:299
  41.3 1.9 %collective-permute-start.5 = (bf16[480,512]{1,0:T(8,128)(2,1)S(1)}, bf16[480,512]{1,0:T(8,128)(2,1)S(1)}, u32[]{:S(2)}, u32[]{:S(2)}) collective-permute-start(bf16[480,512]{1,0:T(8,128)(2,1)S(1)} %fusion.4), channel_id=1, source_target_pairs={{0,2},{1,3},{2,4},{3,5},{4,6},{5,7},{6,8},{7,9},{8,10},{9,11},{10,... | collective-permute-start | bytes 1474568 | tf_op jit(solution)/shard_map/ppermute | solution.py:299
  43.2 9.4 %collective-permute-done.5 = bf16[480,512]{1,0:T(8,128)(2,1)S(1)} collective-permute-done((bf16[480,512]{1,0:T(8,128)(2,1)S(1)}, bf16[480,512]{1,0:T(8,128)(2,1)S(1)}, u32[]{:S(2)}, u32[]{:S(2)}) %collective-permute-start.5) | collective-permute-done | bytes 491552 | tf_op jit(solution)/shard_map/ppermute | solution.py:299
  52.7 3.4 %collective-permute-start.6 = (bf16[480,512]{1,0:T(8,128)(2,1)S(1)}, bf16[480,512]{1,0:T(8,128)(2,1)S(1)}, u32[]{:S(2)}, u32[]{:S(2)}) collective-permute-start(bf16[480,512]{1,0:T(8,128)(2,1)S(1)} %get-tuple-element.10), channel_id=1, source_target_pairs={{0,2},{1,3},{2,4},{3,5},{4,6},{5,7},{6,8},{7,9},{8,10},{9,11},{10,... | collective-permute-start | bytes 1474568 | tf_op jit(solution)/shard_map/ppermute | solution.py:299
  56.2 8.8 %collective-permute-done.9 = bf16[480,512]{1,0:T(8,128)(2,1)S(1)} collective-permute-done((bf16[480,512]{1,0:T(8,128)(2,1)S(1)}, bf16[480,512]{1,0:T(8,128)(2,1)S(1)}, u32[]{:S(2)}, u32[]{:S(2)}) %collective-permute-start.9) | collective-permute-done | bytes 491552 | tf_op jit(solution)/shard_map/ppermute | solution.py:300
  65.1 11.1 %collective-permute-done.10 = bf16[480,512]{1,0:T(8,128)(2,1)S(1)} collective-permute-done((bf16[480,512]{1,0:T(8,128)(2,1)S(1)}, bf16[480,512]{1,0:T(8,128)(2,1)S(1)}, u32[]{:S(2)}, u32[]{:S(2)}) %collective-permute-start.10) | collective-permute-done | bytes 491552 | tf_op jit(solution)/shard_map/ppermute | solution.py:300
  76.5 3.2 %collective-permute-start.11 = (bf16[480,512]{1,0:T(8,128)(2,1)S(1)}, bf16[480,512]{1,0:T(8,128)(2,1)S(1)}, u32[]{:S(2)}, u32[]{:S(2)}) collective-permute-start(bf16[480,512]{1,0:T(8,128)(2,1)S(1)} %fusion.1.r_1_), channel_id=1, source_target_pairs={{0,2},{1,3},{2,4},{3,5},{4,6},{5,7},{6,8},{7,9},{8,10},{9,11},{10,... | collective-permute-start | bytes 1474568 | tf_op jit(solution)/shard_map/ppermute | solution.py:299
  79.7 8.2 %collective-permute-done.12.r_3_ = bf16[480,512]{1,0:T(8,128)(2,1)S(1)} collective-permute-done((bf16[480,512]{1,0:T(8,128)(2,1)S(1)}, bf16[480,512]{1,0:T(8,128)(2,1)S(1)}, u32[]{:S(2)}, u32[]{:S(2)}) %collective-permute-start.12) | collective-permute-done | bytes 491552 | tf_op jit(solution)/shard_map/ppermute | solution.py:300
  87.9 3.2 %collective-permute-start.14 = (bf16[480,512]{1,0:T(8,128)(2,1)S(1)}, bf16[480,512]{1,0:T(8,128)(2,1)S(1)}, u32[]{:S(2)}, u32[]{:S(2)}) collective-permute-start(bf16[480,512]{1,0:T(8,128)(2,1)S(1)} %collective-permute-done.11.r_2_.prev_ref), channel_id=1, source_target_pairs={{0,2},{1,3},{2,4},{3,5},{4,6},{5,7},{6,8},{7,9},{8,10},{9,11},{10,... | collective-permute-start | bytes 1474568 | tf_op jit(solution)/shard_map/ppermute | solution.py:299
  92.4 5.5 %collective-permute-done.13.next2_ref = bf16[480,512]{1,0:T(8,128)(2,1)S(1)} collective-permute-done((bf16[480,512]{1,0:T(8,128)(2,1)S(1)}, bf16[480,512]{1,0:T(8,128)(2,1)S(1)}, u32[]{:S(2)}, u32[]{:S(2)}) %collective-permute-start.13) | collective-permute-done | bytes 491552 | tf_op jit(solution)/shard_map/ppermute | solution.py:300
  99.2 1.1 shard_map.102.early_ref
  100.9 2.2 %shard_map.104 = bf16[16,272,128]{2,1,0:T(8,128)(2,1)} custom-call(s32[2]{0:T(128)S(1)} %pad_add_fusion.1.r_0_.meta, bf16[480,512]{1,0:T(8,128)(2,1)S(1)} %collective-permute-done.11.r_2_.prev_ref, bf16[480,512]{1,0:T(8,128)(2,1)S(1)} %collective-permute-done.13.next2_ref, bf16[480,512]{1,0:T(8,128)(2,1)S(1)} %collective-permute-done.14.prev2_ref, ...), custom_call_target="tpu_custom_call" | custom-call | tf_op jit(solution)/shard_map/pallas_call | solution.py:168
  103.1 7.2 %all-to-all-start = ((bf16[16,272,128]{2,1,0:T(8,128)(2,1)}), bf16[16,272,128]{2,1,0:T(8,128)(2,1)S(1)}, u32[]{:S(2)}, u32[]{:S(2)}) async-start(bf16[16,272,128]{2,1,0:T(8,128)(2,1)} %shard_map.104), calls=%async_computation | async-start | bytes 2228224 | tf_op jit(solution)/shard_map/all_to_all | solution.py:335
  110.2 1.3 dynamic_slice.3
  111.5 17.6 %all-to-all-done = bf16[16,272,128]{2,1,0:T(8,128)(2,1)S(1)} async-done(((bf16[16,272,128]{2,1,0:T(8,128)(2,1)}), bf16[16,272,128]{2,1,0:T(8,128)(2,1)S(1)}, u32[]{:S(2)}, u32[]{:S(2)}) %all-to-all-start) | async-done | bytes 1114144 | tf_op jit(solution)/shard_map/all_to_all | solution.py:335
  129.2 5.2 %collective-permute-start.17 = (bf16[272,128]{1,0:T(8,128)(2,1)S(1)}, bf16[272,128]{1,0:T(8,128)(2,1)S(1)}, u32[]{:S(2)}, u32[]{:S(2)}) collective-permute-start(bf16[272,128]{1,0:T(8,128)(2,1)S(1)} %reduce_sum.12), channel_id=1, source_target_pairs={{0,2},{1,32},{16,3},{17,48},{32,18},{33,33},{48,19},{49,49},{64,22... | collective-permute-start | bytes 208904 | tf_op jit(solution)/shard_map/ppermute | solution.py:339
  134.5 1.9 %collective-permute-start.18 = (bf16[272,128]{1,0:T(8,128)(2,1)S(1)}, bf16[272,128]{1,0:T(8,128)(2,1)S(1)}, u32[]{:S(2)}, u32[]{:S(2)}) collective-permute-start(bf16[272,128]{1,0:T(8,128)(2,1)S(1)} %reduce_sum.12), channel_id=1, source_target_pairs={{0,32},{1,2},{16,48},{17,3},{32,33},{33,18},{48,49},{49,19},{64,46... | collective-permute-start | bytes 208904 | tf_op jit(solution)/shard_map/ppermute | solution.py:340
  136.4 1.2 pad_add_fusion.meta
  137.6 3.7 %collective-permute-done.17.first_ref = bf16[272,128]{1,0:T(8,128)(2,1)S(1)} collective-permute-done((bf16[272,128]{1,0:T(8,128)(2,1)S(1)}, bf16[272,128]{1,0:T(8,128)(2,1)S(1)}, u32[]{:S(2)}, u32[]{:S(2)}) %collective-permute-start.17) | collective-permute-done | bytes 69664 | tf_op jit(solution)/shard_map/ppermute | solution.py:339
  141.2 5.0 %collective-permute-done.18.second_ref = bf16[272,128]{1,0:T(8,128)(2,1)S(1)} collective-permute-done((bf16[272,128]{1,0:T(8,128)(2,1)S(1)}, bf16[272,128]{1,0:T(8,128)(2,1)S(1)}, u32[]{:S(2)}, u32[]{:S(2)}) %collective-permute-start.18) | collective-permute-done | bytes 69664 | tf_op jit(solution)/shard_map/ppermute | solution.py:340
  146.9 2.5 %shard_map.105 = (bf16[2,128,256]{2,1,0:T(8,128)(2,1)}, f32[8,128]{1,0:T(8,128)}) custom-call(s32[35]{0:T(128)} %pad_add_fusion.meta, f32[32]{0:T(128)} %eps_occ.1, s32[2,2]{1,0:T(2,128)} %mask.1, bf16[272,128]{1,0:T(8,128)(2,1)} %copy-done.2, bf16[272,128]{1,0:T(8,128)(2,1)} %copy-done.3, f32[16,128]{1,0:T(8,128)} %bitcast.39), custom_call_target="tpu_custom_call" | custom-call | tf_op jit(solution)/shard_map/pallas_call | solution.py:232
  149.4 1.6 %reshape.13 = bf16[2,128,2,128]{3,2,1,0:T(2,128)(2,1)} reshape(bf16[2,128,256]{2,1,0:T(8,128)(2,1)} %get-tuple-element.8) | data formatting | bytes 262144 | tf_op jit(solution)/shard_map/reshape | solution.py:350
  (46 shorter events, 11.5 us)
Async XLA Ops:
  2.0 1.0 copy-start
  3.1 3.2 %copy-start.1 = (bf16[32,960,128]{2,1,0:T(8,128)(2,1)S(1)}, bf16[32,960,128]{2,1,0:T(8,128)(2,1)}, u32[]{:S(2)}) copy-start(bf16[32,960,128]{2,1,0:T(8,128)(2,1)} %a_ref.11) | copy-start | bytes 23592964
  9.0 22.2 %collective-permute-start = (bf16[5,480,512]{2,1,0:T(8,128)(2,1)S(1)}, bf16[5,480,512]{2,1,0:T(8,128)(2,1)S(1)}, u32[]{:S(2)}, u32[]{:S(2)}) collective-permute-start(bf16[5,480,512]{2,1,0:T(8,128)(2,1)S(1)} %shard_map.95), channel_id=1, source_target_pairs={{0,1},{1,0},{2,3},{3,2},{4,5},{5,4},{6,7},{7,6},{8,9},{9,8},{10,11... | collective-permute-start | bytes 7372808 | tf_op jit(solution)/shard_map/ppermute | solution.py:298
  10.6 9.4 %collective-permute-start.1 = (bf16[2,480,512]{2,1,0:T(8,128)(2,1)S(1)}, bf16[2,480,512]{2,1,0:T(8,128)(2,1)S(1)}, u32[]{:S(2)}, u32[]{:S(2)}) collective-permute-start(bf16[2,480,512]{2,1,0:T(8,128)(2,1)S(1)} %shard_map.97), channel_id=1, source_target_pairs={{0,1},{1,0},{2,3},{3,2},{4,5},{5,4},{6,7},{7,6},{8,9},{9,8},{10,11... | collective-permute-start | bytes 2949128 | tf_op jit(solution)/shard_map/ppermute | solution.py:298
  12.1 3.8 %collective-permute-start.2 = (bf16[1,480,512]{2,1,0:T(8,128)(2,1)S(1)}, bf16[1,480,512]{2,1,0:T(8,128)(2,1)S(1)}, u32[]{:S(2)}, u32[]{:S(2)}) collective-permute-start(bf16[1,480,512]{2,1,0:T(8,128)(2,1)S(1)} %shard_map.99), channel_id=1, source_target_pairs={{0,1},{1,0},{2,3},{3,2},{4,5},{5,4},{6,7},{7,6},{8,9},{9,8},{10,11... | collective-permute-start | bytes 1474568 | tf_op jit(solution)/shard_map/ppermute | solution.py:298
  16.8 8.7 %collective-permute-start.3 = (bf16[240,512]{1,0:T(8,128)(2,1)S(1)}, bf16[240,512]{1,0:T(8,128)(2,1)S(1)}, u32[]{:S(2)}, u32[]{:S(2)}) collective-permute-start(bf16[240,512]{1,0:T(8,128)(2,1)S(1)} %get-tuple-element.6), channel_id=1, source_target_pairs={{0,2},{1,3},{2,4},{3,5},{4,6},{5,7},{6,8},{7,9},{8,10},{9,11},{10,... | collective-permute-start | bytes 737288 | tf_op jit(solution)/shard_map/ppermute | solution.py:299
  20.0 8.9 %collective-permute-start.7 = (bf16[240,512]{1,0:T(8,128)(2,1)S(1)}, bf16[240,512]{1,0:T(8,128)(2,1)S(1)}, u32[]{:S(2)}, u32[]{:S(2)}) collective-permute-start(bf16[240,512]{1,0:T(8,128)(2,1)S(1)} %get-tuple-element.7), channel_id=1, source_target_pairs={{0,14},{1,15},{2,0},{3,1},{4,2},{5,3},{6,4},{7,5},{8,6},{9,7},{10,... | collective-permute-start | bytes 737288 | tf_op jit(solution)/shard_map/ppermute | solution.py:300
  29.0 12.2 %collective-permute-start.4 = (bf16[480,512]{1,0:T(8,128)(2,1)S(1)}, bf16[480,512]{1,0:T(8,128)(2,1)S(1)}, u32[]{:S(2)}, u32[]{:S(2)}) collective-permute-start(bf16[480,512]{1,0:T(8,128)(2,1)S(1)} %pad_maximum_fusion), channel_id=1, source_target_pairs={{0,2},{1,3},{2,4},{3,5},{4,6},{5,7},{6,8},{7,9},{8,10},{9,11},{10,... | collective-permute-start | bytes 1474568 | tf_op jit(solution)/shard_map/ppermute | solution.py:299
  29.4 13.7 %collective-permute-start.8 = (bf16[480,512]{1,0:T(8,128)(2,1)S(1)}, bf16[480,512]{1,0:T(8,128)(2,1)S(1)}, u32[]{:S(2)}, u32[]{:S(2)}) collective-permute-start(bf16[480,512]{1,0:T(8,128)(2,1)S(1)} %pad_maximum_fusion.1), channel_id=1, source_target_pairs={{0,14},{1,15},{2,0},{3,1},{4,2},{5,3},{6,4},{7,5},{8,6},{9,7},{10,... | collective-permute-start | bytes 1474568 | tf_op jit(solution)/shard_map/ppermute | solution.py:300
  41.3 11.3 %collective-permute-start.5 = (bf16[480,512]{1,0:T(8,128)(2,1)S(1)}, bf16[480,512]{1,0:T(8,128)(2,1)S(1)}, u32[]{:S(2)}, u32[]{:S(2)}) collective-permute-start(bf16[480,512]{1,0:T(8,128)(2,1)S(1)} %fusion.4), channel_id=1, source_target_pairs={{0,2},{1,3},{2,4},{3,5},{4,6},{5,7},{6,8},{7,9},{8,10},{9,11},{10,... | collective-permute-start | bytes 1474568 | tf_op jit(solution)/shard_map/ppermute | solution.py:299
  52.7 12.3 %collective-permute-start.9 = (bf16[480,512]{1,0:T(8,128)(2,1)S(1)}, bf16[480,512]{1,0:T(8,128)(2,1)S(1)}, u32[]{:S(2)}, u32[]{:S(2)}) collective-permute-start(bf16[480,512]{1,0:T(8,128)(2,1)S(1)} %get-tuple-element.11), channel_id=1, source_target_pairs={{0,14},{1,15},{2,0},{3,1},{4,2},{5,3},{6,4},{7,5},{8,6},{9,7},{10,... | collective-permute-start | bytes 1474568 | tf_op jit(solution)/shard_map/ppermute | solution.py:300
  52.7 12.3 %collective-permute-start.6 = (bf16[480,512]{1,0:T(8,128)(2,1)S(1)}, bf16[480,512]{1,0:T(8,128)(2,1)S(1)}, u32[]{:S(2)}, u32[]{:S(2)}) collective-permute-start(bf16[480,512]{1,0:T(8,128)(2,1)S(1)} %get-tuple-element.10), channel_id=1, source_target_pairs={{0,2},{1,3},{2,4},{3,5},{4,6},{5,7},{6,8},{7,9},{8,10},{9,11},{10,... | collective-permute-start | bytes 1474568 | tf_op jit(solution)/shard_map/ppermute | solution.py:299
  65.0 11.2 %collective-permute-start.10 = (bf16[480,512]{1,0:T(8,128)(2,1)S(1)}, bf16[480,512]{1,0:T(8,128)(2,1)S(1)}, u32[]{:S(2)}, u32[]{:S(2)}) collective-permute-start(bf16[480,512]{1,0:T(8,128)(2,1)S(1)} %fusion.3), channel_id=1, source_target_pairs={{0,14},{1,15},{2,0},{3,1},{4,2},{5,3},{6,4},{7,5},{8,6},{9,7},{10,... | collective-permute-start | bytes 1474568 | tf_op jit(solution)/shard_map/ppermute | solution.py:300
  76.4 11.5 %collective-permute-start.12 = (bf16[480,512]{1,0:T(8,128)(2,1)S(1)}, bf16[480,512]{1,0:T(8,128)(2,1)S(1)}, u32[]{:S(2)}, u32[]{:S(2)}) collective-permute-start(bf16[480,512]{1,0:T(8,128)(2,1)S(1)} %fusion.1.r_1_), channel_id=1, source_target_pairs={{0,14},{1,15},{2,0},{3,1},{4,2},{5,3},{6,4},{7,5},{8,6},{9,7},{10,... | collective-permute-start | bytes 1474568 | tf_op jit(solution)/shard_map/ppermute | solution.py:300
  76.5 11.4 %collective-permute-start.11 = (bf16[480,512]{1,0:T(8,128)(2,1)S(1)}, bf16[480,512]{1,0:T(8,128)(2,1)S(1)}, u32[]{:S(2)}, u32[]{:S(2)}) collective-permute-start(bf16[480,512]{1,0:T(8,128)(2,1)S(1)} %fusion.1.r_1_), channel_id=1, source_target_pairs={{0,2},{1,3},{2,4},{3,5},{4,6},{5,7},{6,8},{7,9},{8,10},{9,11},{10,... | collective-permute-start | bytes 1474568 | tf_op jit(solution)/shard_map/ppermute | solution.py:299
  87.9 10.0 %collective-permute-start.13 = (bf16[480,512]{1,0:T(8,128)(2,1)S(1)}, bf16[480,512]{1,0:T(8,128)(2,1)S(1)}, u32[]{:S(2)}, u32[]{:S(2)}) collective-permute-start(bf16[480,512]{1,0:T(8,128)(2,1)S(1)} %collective-permute-done.12.r_3_), channel_id=1, source_target_pairs={{0,14},{1,15},{2,0},{3,1},{4,2},{5,3},{6,4},{7,5},{8,6},{9,7},{10,... | collective-permute-start | bytes 1474568 | tf_op jit(solution)/shard_map/ppermute | solution.py:300
  87.9 10.0 %collective-permute-start.14 = (bf16[480,512]{1,0:T(8,128)(2,1)S(1)}, bf16[480,512]{1,0:T(8,128)(2,1)S(1)}, u32[]{:S(2)}, u32[]{:S(2)}) collective-permute-start(bf16[480,512]{1,0:T(8,128)(2,1)S(1)} %collective-permute-done.11.r_2_.prev_ref), channel_id=1, source_target_pairs={{0,2},{1,3},{2,4},{3,5},{4,6},{5,7},{6,8},{7,9},{8,10},{9,11},{10,... | collective-permute-start | bytes 1474568 | tf_op jit(solution)/shard_map/ppermute | solution.py:299
  92.3 6.8 %collective-permute-start.15 = (bf16[10,272,128]{2,1,0:T(8,128)(2,1)S(1)}, bf16[10,272,128]{2,1,0:T(8,128)(2,1)S(1)}, u32[]{:S(2)}, u32[]{:S(2)}) collective-permute-start(bf16[10,272,128]{2,1,0:T(8,128)(2,1)S(1)} %shard_map.101), channel_id=1, source_target_pairs={{0,1},{1,0},{2,3},{3,2},{4,5},{5,4},{6,7},{7,6},{8,9},{9,8},{10,11... | collective-permute-start | bytes 2088968 | tf_op jit(solution)/shard_map/ppermute | solution.py:298
  99.0 1.8 %collective-permute-start.16 = (bf16[6,272,128]{2,1,0:T(8,128)(2,1)S(1)}, bf16[6,272,128]{2,1,0:T(8,128)(2,1)S(1)}, u32[]{:S(2)}, u32[]{:S(2)}) collective-permute-start(bf16[6,272,128]{2,1,0:T(8,128)(2,1)S(1)} %shard_map.103), channel_id=1, source_target_pairs={{0,1},{1,0},{2,3},{3,2},{4,5},{5,4},{6,7},{7,6},{8,9},{9,8},{10,11... | collective-permute-start | bytes 1253384 | tf_op jit(solution)/shard_map/ppermute | solution.py:298
  103.1 33.3 %copy-start.4 = (s32[32]{0:T(128)S(1)}, s32[32]{0:T(128)}, u32[]{:S(2)}) copy-start(s32[32]{0:T(128)} %param.10) | copy-start | bytes 388
  103.1 26.0 %all-to-all-start = ((bf16[16,272,128]{2,1,0:T(8,128)(2,1)}), bf16[16,272,128]{2,1,0:T(8,128)(2,1)S(1)}, u32[]{:S(2)}, u32[]{:S(2)}) async-start(bf16[16,272,128]{2,1,0:T(8,128)(2,1)} %shard_map.104), calls=%async_computation | async-start | bytes 2228224 | tf_op jit(solution)/shard_map/all_to_all | solution.py:335
  129.2 12.0 %collective-permute-start.17 = (bf16[272,128]{1,0:T(8,128)(2,1)S(1)}, bf16[272,128]{1,0:T(8,128)(2,1)S(1)}, u32[]{:S(2)}, u32[]{:S(2)}) collective-permute-start(bf16[272,128]{1,0:T(8,128)(2,1)S(1)} %reduce_sum.12), channel_id=1, source_target_pairs={{0,2},{1,32},{16,3},{17,48},{32,18},{33,33},{48,19},{49,49},{64,22... | collective-permute-start | bytes 208904 | tf_op jit(solution)/shard_map/ppermute | solution.py:339
  134.5 11.8 %collective-permute-start.18 = (bf16[272,128]{1,0:T(8,128)(2,1)S(1)}, bf16[272,128]{1,0:T(8,128)(2,1)S(1)}, u32[]{:S(2)}, u32[]{:S(2)}) collective-permute-start(bf16[272,128]{1,0:T(8,128)(2,1)S(1)} %reduce_sum.12), channel_id=1, source_target_pairs={{0,32},{1,2},{16,48},{17,3},{32,33},{33,18},{48,49},{49,19},{64,46... | collective-permute-start | bytes 208904 | tf_op jit(solution)/shard_map/ppermute | solution.py:340
  141.2 5.0 %copy-start.2 = (bf16[272,128]{1,0:T(8,128)(2,1)}, bf16[272,128]{1,0:T(8,128)(2,1)S(1)}, u32[]{:S(2)}) copy-start(bf16[272,128]{1,0:T(8,128)(2,1)S(1)} %collective-permute-done.17.first_ref) | copy-start | bytes 208900
  146.2 0.6 copy-start.3

commit v2 on v1

v2 whole, which is shorter than its diff:
```python
import functools

import jax
import jax.numpy as jnp
import numpy as np
from jax import lax
from jax.experimental import pallas as pl
from jax.experimental.pallas import tpu as pltpu
from jax.sharding import PartitionSpec as P

NAUX = 15360
BS = 128
CHIPS = 8
OWN = 4
EXTRA = 16
ROWS = 2 * BS + EXTRA
EARLY = 10
SLOTS = 16
RINGS = 2
TRANSFORM_VMEM = 24 * 2**20
PAIR_VMEM = 32 * 2**20


def transform_rows(out_ref, rows, a_at, coeff_at):
    for q in range(OWN):
        out_ref[:, q * BS : (q + 1) * BS] = jnp.dot(
            a_at(q, rows), coeff_at(q), preferred_element_type=jnp.float32
        ).astype(out_ref.dtype)


def core_halves():
    core = lax.axis_index("orb") % 2
    return 1 - core, core


def transform_kernel(firsts, domains, a_hbm, c_hbm, send_ref, own_ref, a_ref, c_ref, sems):
    copies = []
    for n, first in enumerate(firsts):
        chunk = (lax.axis_index("orb") // 2 + first) % CHIPS
        here = []
        for q in range(OWN):
            lanes = pl.ds(pl.multiple_of(domains[OWN * chunk + q] * BS, BS), BS)
            here.append((c_hbm.at[:, lanes], c_ref.at[n, q]))
        for side, half in enumerate(core_halves()):
            here.append((a_hbm.at[pl.ds(OWN * chunk, OWN), half], a_ref.at[n, side]))
        copies.append(
            [pltpu.make_async_copy(x, y, sems.at[n, k]) for k, (x, y) in enumerate(here)]
        )
        for copy in copies[-1]:
            copy.start()
    for n in range(len(firsts)):
        for copy in copies[n][:-1]:
            copy.wait()
        transform_rows(send_ref.at[n], 0, lambda q, side: a_ref[n, side, q], lambda q: c_ref[n, q])
        copies[n][-1].wait()
        transform_rows(own_ref.at[n], 1, lambda q, side: a_ref[n, side, q], lambda q: c_ref[n, q])


def transform_call(domains, integrals, coeffs, firsts):
    half, width, count = integrals.shape[2], OWN * BS, len(firsts)
    hbm = pl.BlockSpec(memory_space=pltpu.HBM)
    vmem = pl.BlockSpec(memory_space=pltpu.VMEM)
    return pl.pallas_call(
        functools.partial(transform_kernel, firsts),
        in_specs=[pl.BlockSpec(memory_space=pltpu.SMEM), hbm, hbm],
        out_specs=(vmem, vmem),
        scratch_shapes=[
            pltpu.VMEM((count, 2, OWN, half, BS), jnp.bfloat16),
            pltpu.VMEM((count, OWN, BS, BS), jnp.bfloat16),
            pltpu.SemaphoreType.DMA((count, OWN + 2)),
        ],
        out_shape=(
            jax.ShapeDtypeStruct((count, half, width), jnp.bfloat16),
            jax.ShapeDtypeStruct((count, half, width), jnp.float32),
        ),
        cost_estimate=pl.CostEstimate(
            flops=4 * count * half * width * BS,
            bytes_accessed=count * half * (4 * width + 6 * width),
            transcendentals=0,
        ),
        compiler_params=pltpu.CompilerParams(vmem_limit_bytes=TRANSFORM_VMEM),
    )(domains, integrals, coeffs)


def gram(left, right):
    return lax.dot_general(
        left, right, (((0,), (0,)), ((), ())), preferred_element_type=jnp.float32
    )


def orbital(ref, index):
    return ref[:, pl.ds(pl.multiple_of(index * BS, BS), BS)]


def put(out_ref, slot, product, received):
    for m in range(2):
        value = product[:, m * BS : (m + 1) * BS]
        if received is not None:
            value = value + received[slot, m * BS : (m + 1) * BS].astype(jnp.float32)
        out_ref[slot, m * BS : (m + 1) * BS] = value.astype(jnp.bfloat16)
    out_ref[slot, 2 * BS :] = jnp.zeros((EXTRA, BS), jnp.bfloat16)


def block_products(h, left_ref, right_ref, slot, out_ref, received):
    left = jnp.concatenate([orbital(left_ref, h), orbital(left_ref, 2 + h)], axis=1)
    product = gram(left, right_ref[...])
    for l in range(2):
        for m in range(2):
            piece = product[l * BS : (l + 1) * BS, 2 * m * BS : 2 * (m + 1) * BS]
            put(out_ref, slot + 2 * l + m, piece, received)


def early_kernel(other, own_ref, prev_ref, next_ref, *refs):
    received, out_ref = refs if len(refs) == 2 else (None, refs[0])
    core = lax.axis_index("orb") % 2
    h = 1 - core if other else core
    block_products(h, own_ref, next_ref, 0, out_ref, received)
    block_products(h, prev_ref, next_ref, 4, out_ref, received)
    put(out_ref, 8, gram(orbital(own_ref, h), own_ref[:, 2 * BS :]), received)
    pair = jnp.concatenate([orbital(own_ref, 2 * h), orbital(own_ref, 2 * h + 1)], axis=1)
    diag = gram(pair, pair)
    row = lax.broadcasted_iota(jnp.int32, (BS, BS), 0)
    col = lax.broadcasted_iota(jnp.int32, (BS, BS), 1)
    second = diag[BS:, BS:]
    packed = jnp.where(row >= col, diag[:BS, :BS], second)
    line = jnp.sum(jnp.where(row == col, second, 0.0), axis=0, keepdims=True)
    line = jnp.broadcast_to(line, (EXTRA, BS))
    cross = diag[:BS, BS:]
    if received is not None:
        packed = packed + received[9, :BS].astype(jnp.float32)
        cross = cross + received[9, BS : 2 * BS].astype(jnp.float32)
        line = line + received[9, 2 * BS :].astype(jnp.float32)
    out_ref[9, :BS] = packed.astype(jnp.bfloat16)
    out_ref[9, BS : 2 * BS] = cross.astype(jnp.bfloat16)
    out_ref[9, 2 * BS :] = line.astype(jnp.bfloat16)


def late_products(other, prev_ref, next2_ref, prev2_ref, slot, out_ref, received):
    core = lax.axis_index("orb") % 2
    chip = lax.axis_index("orb") // 2
    h = 1 - core if other else core
    block_products(h, prev_ref, next2_ref, slot, out_ref, received)

    def opposite(left, right):
        product = gram(left, right[...])
        for m in range(2):
            put(out_ref, slot + 4 + m, product[:, 2 * m * BS : 2 * (m + 1) * BS], received)

    @pl.when(chip < CHIPS // 2)
    def _():
        opposite(orbital(prev2_ref, h), next2_ref)

    @pl.when(chip >= CHIPS // 2)
    def _():
        opposite(orbital(next2_ref, 2 + h), prev2_ref)


def late_send_kernel(prev_ref, next2_ref, prev2_ref, out_ref):
    late_products(True, prev_ref, next2_ref, prev2_ref, 0, out_ref, None)


class Shifted:
    def __init__(self, ref, by):
        self.ref, self.by = ref, by

    def __getitem__(self, key):
        return self.ref[(key[0] - self.by,) + key[1:]]


def late_own_kernel(prev_ref, next2_ref, prev2_ref, early_ref, received, out_ref):
    out_ref[:EARLY] = early_ref[...]
    late_products(
        False, prev_ref, next2_ref, prev2_ref, EARLY, out_ref, Shifted(received, EARLY)
    )


def pair_call(body, operands, slots):
    return pl.pallas_call(
        body,
        out_shape=jax.ShapeDtypeStruct((slots, ROWS, BS), jnp.bfloat16),
        compiler_params=pltpu.CompilerParams(vmem_limit_bytes=PAIR_VMEM),
    )(*operands)


def final_kernel(kinds, domains, eps_occ, mask, both_ref, vir_ref, amp_ref, energy_ref, t_ref):
    first_ref, second_ref = both_ref.at[:ROWS], both_ref.at[ROWS:]
    aux = lax.axis_index("aux")
    orb = lax.axis_index("orb")
    kind = kinds[aux, orb]
    units = [slice(0, BS), slice(BS, 2 * BS)]

    @pl.when(kind == 0)
    def _():
        for j, ref in enumerate((first_ref, second_ref)):
            for i in range(2):
                t_ref[j, i] = ref[units[i]].astype(jnp.float32)

    @pl.when(kind == 1)
    def _():
        for i, ref in enumerate((second_ref, first_ref)):
            for j in range(2):
                t_ref[j, i] = ref[units[j]].astype(jnp.float32).T

    @pl.when(kind == 2)
    def _():
        row = lax.broadcasted_iota(jnp.int32, (BS, BS), 0)
        col = lax.broadcasted_iota(jnp.int32, (BS, BS), 1)
        packed = first_ref[units[0]].astype(jnp.float32)
        flipped = packed.T
        line = first_ref[2 * BS : 2 * BS + EXTRA].astype(jnp.float32)[:1]
        t_ref[0, 0] = jnp.where(row >= col, packed, flipped)
        t_ref[1, 1] = jnp.where(row < col, packed, jnp.where(row > col, flipped, line))
        cross = first_ref[units[1]].astype(jnp.float32)
        t_ref[0, 1] = cross
        t_ref[1, 0] = cross.T

    scale = 1.0 / np.sqrt(np.float32(NAUX))
    for j in range(2):
        jj = 2 * aux + j
        vir_j = vir_ref[pl.ds(domains[jj], 1), :]
        rows = jnp.broadcast_to(vir_j, (BS, BS)).T
        amps = []
        for i in range(2):
            ii = 2 * orb + i
            vir_i = vir_ref[pl.ds(domains[ii], 1), :]
            denominator = rows + vir_i - eps_occ[jj] - eps_occ[ii]
            pair = t_ref[j, i] * scale
            keep = mask[j, i].astype(jnp.float32)
            amp = keep * pair / denominator
            amps.append(amp)
            energy_ref[j, i] = jnp.sum(pair * amp) * (-1.0 / (BS * BS))
        amp_ref[j] = jnp.stack(amps, axis=1).astype(jnp.bfloat16)


def final_call(kinds, domains, eps_occ, mask, both, vir):
    return pl.pallas_call(
        final_kernel,
        grid_spec=pltpu.PrefetchScalarGridSpec(
            num_scalar_prefetch=4,
            grid=(1,),
            in_specs=[
                pl.BlockSpec(both.shape, lambda n, *m: (0, 0)),
                pl.BlockSpec(vir.shape, lambda n, *m: (0, 0)),
            ],
            out_specs=(
                pl.BlockSpec((2, BS, 2, BS), lambda n, *m: (0, 0, 0, 0)),
                pl.BlockSpec(memory_space=pltpu.SMEM),
            ),
            scratch_shapes=[pltpu.VMEM((2, 2, BS, BS), jnp.float32)],
        ),
        out_shape=(
            jax.ShapeDtypeStruct((2, BS, 2, BS), jnp.bfloat16),
            jax.ShapeDtypeStruct((2, 2), jnp.float32),
        ),
        compiler_params=pltpu.CompilerParams(vmem_limit_bytes=PAIR_VMEM),
    )(kinds, domains, eps_occ, mask, both, vir)


def slot_pairs(chip):
    sup = lambda off, l: 2 * ((chip + off) % CHIPS) + l
    pairs = [(sup(0, l), sup(1, m)) for l in range(2) for m in range(2)]
    pairs += [(sup(-1, l), sup(1, m)) for l in range(2) for m in range(2)]
    pairs += [(sup(0, 0), sup(0, 1)), None]
    pairs += [(sup(-1, l), sup(2, m)) for l in range(2) for m in range(2)]
    if chip < CHIPS // 2:
        pairs += [(sup(-2, 0), sup(2, m)) for m in range(2)]
    else:
        pairs += [(sup(2, 1), sup(-2, m)) for m in range(2)]
    return pairs


def delivery():
    pairs = []
    kind = np.full((SLOTS, SLOTS), -1, np.int32)
    for chip in range(CHIPS):
        for slot, pair in enumerate(slot_pairs(chip)):
            for core in range(2):
                u, v = pair or (2 * chip + core,) * 2
                owner = (v, u) if core else (u, v)
                pairs.append((slot * SLOTS + 2 * chip + core, owner[0] * SLOTS + owner[1]))
                kind[owner] = core if pair else 2
    assert (kind >= 0).all()
    return pairs, kind


def shards(integrals, coeffs, domains, eps_occ, eps_vir, pair_mask):
    f32 = jnp.float32
    half = integrals.shape[1] // 2
    integrals = integrals.reshape(-1, 2, half, BS)
    n_orb = 2 * CHIPS
    tie = lax.optimization_barrier
    swap = lambda x: lax.ppermute(x, "orb", [(o, o ^ 1) for o in range(n_orb)])
    up = lambda x: lax.ppermute(x, "orb", [(o, (o + 2) % n_orb) for o in range(n_orb)])
    down = lambda x: lax.ppermute(x, "orb", [(o, (o - 2) % n_orb) for o in range(n_orb)])

    part = half // RINGS
    terms = {}

    def after(x, *others):
        return tie((x, *others))[0]

    def transform(firsts, *others):
        send, mine = transform_call(domains, after(integrals, *others), coeffs, firsts)
        theirs = swap(send)
        values = [
            mine[n, first : first + part] + theirs[n, first : first + part].astype(f32)
            for n in range(len(firsts))
            for first in range(0, half, part)
        ]
        if len(firsts) > 1:
            values = tie(values)
        terms.update({k: values[RINGS * n : RINGS * (n + 1)] for n, k in enumerate(firsts)})
        return send

    def add(x, *received):
        return sum((r.astype(f32) for r in received), x).astype(jnp.bfloat16)

    send = transform((4,))
    send = transform((3, 5), send)
    transform((2, 6, 1, 7, 0), send)
    h = part // 2
    starts = [tie((add(x[:h]), add(x[h:]))) for x in terms[4]]
    sums = [(up(u), down(d)) for u, d in starts]
    for step in (3, 2, 1):
        later = []
        for n, (u, d) in enumerate(sums):
            x, y = terms[step][n], terms[CHIPS - step][n]
            if step == 3:
                u = jnp.concatenate([add(x[:h], u), add(x[h:])], axis=0)
                d = jnp.concatenate([add(y[:h]), add(y[h:], d)], axis=0)
            else:
                u, d = add(x, u), add(y, d)
            u, d = tie((u, d))
            later.append((up(u), down(d)))
        sums = later
    own, prev, next_, prev2, next2 = [], [], [], [], []
    for n, (u, d) in enumerate(sums):
        own.append(tie(add(terms[0][n], u, d)))
        prev.append(up(own[-1]))
        next_.append(down(own[-1]))
    for n in range(RINGS):
        u, d = tie((prev[n], next_[n]))
        prev2.append(up(u))
        next2.append(down(d))
    own, prev, next_, prev2, next2 = (
        jnp.concatenate(x, axis=0) for x in (own, prev, next_, prev2, next2)
    )

    send = pair_call(functools.partial(early_kernel, True), (own, prev, next_), EARLY)
    early = pair_call(
        functools.partial(early_kernel, False), (own, prev, next_, swap(send)), EARLY
    )
    send = pair_call(late_send_kernel, (prev, next2, prev2), SLOTS - EARLY)
    sums = pair_call(late_own_kernel, (prev, next2, prev2, early, swap(send)), SLOTS)
    parts = lax.all_to_all(sums.reshape(SLOTS * ROWS, BS), "aux", 0, 0, tiled=True)
    held = jnp.sum(parts.reshape(SLOTS, ROWS, BS).astype(f32), axis=0).astype(jnp.bfloat16)
    both = jnp.concatenate([held, swap(held)], axis=0)
    pairs, kind = delivery()
    both = lax.ppermute(both, ("aux", "orb"), pairs)
    return final_call(
        jnp.asarray(kind), domains, eps_occ, pair_mask, both, eps_vir.reshape(-1, BS)
    )


def solution(mesh):
    return jax.shard_map(
        shards,
        mesh=mesh,
        in_specs=(P(None, "aux", "orb"), P("orb", None), P(), P(), P(), P("aux", "orb")),
        out_specs=(P("aux", None, "orb", None), P("aux", "orb")),
        check_vma=False,
    )
```

time: 154 us -> 133 us (0.86)
  waiting for transfers between devices: 88.2 us -> 46.1 us
  blocking collectives: 0 us -> 25.1 us
  starting transfers between devices: 32.7 us -> 38.9 us
  Pallas kernels: 18.1 us -> 12.6 us
  local copies, waits for them, and re-layouts: 9.24 us -> 5.21 us
    all_to_all x0 -> x1, blocking collectives: none -> 25.1 us  [shards(): lax.all_to_all(sums.reshape(SLOTS * ROWS, BS), 'aux', 0, 0, tiled=True)]
    all_to_all x1 -> x0, waiting for transfers between devices: 17.6 us -> none  [shards(): parts = lax.all_to_all(sums, 'aux', 0, 0, tiled=True)]
    ppermute x6 -> x12, waiting for transfers between devices: 36.9 us -> 25 us  [shards(): lax.ppermute(x, 'orb', [(o, (o - 2) % n_orb) for o in range(n_orb)])]
    ppermute x6 -> x12, waiting for transfers between devices: 20.6 us -> 10.5 us  [shards(): lax.ppermute(x, 'orb', [(o, (o + 2) % n_orb) for o in range(n_orb)])]
    ppermute x6 -> x12, starting transfers between devices: 2.07 us -> 12 us  [shards(): lax.ppermute(x, 'orb', [(o, (o - 2) % n_orb) for o in range(n_orb)])]
    all_to_all x1 -> x0, starting transfers between devices: 7.15 us -> none  [shards(): parts = lax.all_to_all(sums, 'aux', 0, 0, tiled=True)]
    pallas_call x10 -> x7, Pallas kernels: 15.6 us -> 10.9 us  [the longest x3 8.46 us: transform_call(): pl.pallas_call(functools.partial(transform_kernel, firsts), in_specs=[pl....]
    ppermute x6 -> x12, starting transfers between devices: 15.4 us -> 20 us  [shards(): lax.ppermute(x, 'orb', [(o, (o + 2) % n_orb) for o in range(n_orb)])]
  transfers between devices with their start and end apart: 20 -> 31, of which waited for: 13 -> 17; matrix products, arithmetic and copies ran while one was open for 2% -> 2% of each run, Pallas kernels for 7% -> 7%
where the time goes in v2:
time: 133 us; the launch traced here: 132 us
  waiting for transfers between devices  46.1 us (35%)
  starting transfers between devices  38.9 us (29%)
  blocking collectives  25.1 us (19%)
  Pallas kernels  12.6 us (9%)
  local copies, waits for them, and re-layouts  5.21 us (4%)
  other arithmetic  2.51 us (2%)
    all_to_all x1, blocking collectives, shards(): lax.all_to_all(sums.reshape(SLOTS * ROWS, BS), 'aux', 0, 0, tiled=True)  25.1 us
    ppermute x12, waiting for transfers between devices, shards(): lax.ppermute(x, 'orb', [(o, (o - 2) % n_orb) for o in range(n_orb)])  25 us
    ppermute x12, starting transfers between devices, shards(): lax.ppermute(x, 'orb', [(o, (o + 2) % n_orb) for o in range(n_orb)])  20 us
    ppermute x12, starting transfers between devices, shards(): lax.ppermute(x, 'orb', [(o, (o - 2) % n_orb) for o in range(n_orb)])  12 us
    ppermute x12, waiting for transfers between devices, shards(): lax.ppermute(x, 'orb', [(o, (o + 2) % n_orb) for o in range(n_orb)])  10.5 us
    pallas_call x3, Pallas kernels, transform_call(): pl.pallas_call(functools.partial(transform_kernel, firsts), in_specs=[pl....  8.46 us
    ppermute x1, waiting for transfers between devices, shards(): both = lax.ppermute(both, ('aux', 'orb'), pairs)  8.11 us
    ppermute x1, starting transfers between devices, shards(): both = lax.ppermute(both, ('aux', 'orb'), pairs)  5.77 us
  transfers between devices with their start and end apart: 31, of which 17 were waited for; matrix products, arithmetic and copies ran while one was open for 2% of the time, Pallas kernels for 7%

profile of v2, /device:TPU:96, one launch (start us, length us, event | category | flops | bytes accessed | tf_op | source)
XLA Modules:
  0.0 131.7 jit_solution(6394389955459451289)
XLA Ops:
  0.6 3.2 %copy-done = bf16[32,960,128]{2,1,0:T(8,128)(2,1)S(1)} copy-done((bf16[32,960,128]{2,1,0:T(8,128)(2,1)S(1)}, bf16[32,960,128]{2,1,0:T(8,128)(2,1)}, u32[]{:S(2)}) %copy-start) | copy-done | bytes 7864344
  5.6 1.4 %shard_map.86 = (bf16[1,480,512]{2,1,0:T(8,128)(2,1)S(1)}, f32[1,480,512]{2,1,0:T(8,128)S(1)}) custom-call(s32[32]{0:T(128)S(1)} %copy-done.2, bf16[32,2,480,128]{3,2,1,0:T(8,128)(2,1)S(1)} %bitcast.38, bf16[128,2048]{1,0:T(8,128)(2,1)S(1)} %copy-done.1), custom_call_target="tpu_custom_call" | custom-call | flops 125829120 | bytes 2457600 | tf_op jit(solution)/shard_map/pallas_call | solution.py:63
  7.1 2.3 %shard_map.87 = (bf16[2,480,512]{2,1,0:T(8,128)(2,1)S(1)}, f32[2,480,512]{2,1,0:T(8,128)S(1)}) custom-call(s32[32]{0:T(128)S(1)} %copy-done.2, bf16[32,2,480,128]{3,2,1,0:T(8,128)(2,1)S(1)} %bitcast.39, bf16[128,2048]{1,0:T(8,128)(2,1)S(1)} %copy-done.1), custom_call_target="tpu_custom_call" | custom-call | flops 251658240 | bytes 4915200 | tf_op jit(solution)/shard_map/pallas_call | solution.py:63
  9.9 4.8 %shard_map.88 = (bf16[5,480,512]{2,1,0:T(8,128)(2,1)S(1)}, f32[5,480,512]{2,1,0:T(8,128)S(1)}) custom-call(s32[32]{0:T(128)S(1)} %copy-done.2, bf16[32,2,480,128]{3,2,1,0:T(8,128)(2,1)S(1)} %bitcast.40, bf16[128,2048]{1,0:T(8,128)(2,1)S(1)} %copy-done.1), custom_call_target="tpu_custom_call" | custom-call | flops 629145600 | bytes 12288000 | tf_op jit(solution)/shard_map/pallas_call | solution.py:63
  15.0 3.2 %collective-permute-start.3 = (bf16[120,512]{1,0:T(8,128)(2,1)S(1)}, bf16[120,512]{1,0:T(8,128)(2,1)S(1)}, u32[]{:S(2)}, u32[]{:S(2)}) collective-permute-start(bf16[120,512]{1,0:T(8,128)(2,1)S(1)} %get-tuple-element.56), channel_id=1, source_target_pairs={{0,2},{1,3},{2,4},{3,5},{4,6},{5,7},{6,8},{7,9},{8,10},{9,11},{10,... | collective-permute-start | bytes 368648 | tf_op jit(solution)/shard_map/ppermute | solution.py:293
  18.3 3.2 %collective-permute-start.12 = (bf16[120,512]{1,0:T(8,128)(2,1)S(1)}, bf16[120,512]{1,0:T(8,128)(2,1)S(1)}, u32[]{:S(2)}, u32[]{:S(2)}) collective-permute-start(bf16[120,512]{1,0:T(8,128)(2,1)S(1)} %get-tuple-element.71), channel_id=1, source_target_pairs={{0,2},{1,3},{2,4},{3,5},{4,6},{5,7},{6,8},{7,9},{8,10},{9,11},{10,... | collective-permute-start | bytes 368648 | tf_op jit(solution)/shard_map/ppermute | solution.py:293
  21.8 2.3 %collective-permute-done.12 = bf16[120,512]{1,0:T(8,128)(2,1)S(1)} collective-permute-done((bf16[120,512]{1,0:T(8,128)(2,1)S(1)}, bf16[120,512]{1,0:T(8,128)(2,1)S(1)}, u32[]{:S(2)}, u32[]{:S(2)}) %collective-permute-start.12) | collective-permute-done | bytes 122912 | tf_op jit(solution)/shard_map/ppermute | solution.py:293
  24.2 3.4 %collective-permute-done.13 = bf16[120,512]{1,0:T(8,128)(2,1)S(1)} collective-permute-done((bf16[120,512]{1,0:T(8,128)(2,1)S(1)}, bf16[120,512]{1,0:T(8,128)(2,1)S(1)}, u32[]{:S(2)}, u32[]{:S(2)}) %collective-permute-start.13) | collective-permute-done | bytes 122912 | tf_op jit(solution)/shard_map/ppermute | solution.py:294
  28.3 1.7 %collective-permute-start.6 = (bf16[240,512]{1,0:T(8,128)(2,1)S(1)}, bf16[240,512]{1,0:T(8,128)(2,1)S(1)}, u32[]{:S(2)}, u32[]{:S(2)}) collective-permute-start(bf16[240,512]{1,0:T(8,128)(2,1)S(1)} %pad_maximum_fusion.2), channel_id=1, source_target_pairs={{0,14},{1,15},{2,0},{3,1},{4,2},{5,3},{6,4},{7,5},{8,6},{9,7},{10,... | collective-permute-start | bytes 737288 | tf_op jit(solution)/shard_map/ppermute | solution.py:294
  30.0 1.5 %collective-permute-start.14 = (bf16[240,512]{1,0:T(8,128)(2,1)S(1)}, bf16[240,512]{1,0:T(8,128)(2,1)S(1)}, u32[]{:S(2)}, u32[]{:S(2)}) collective-permute-start(bf16[240,512]{1,0:T(8,128)(2,1)S(1)} %pad_maximum_fusion.3), channel_id=1, source_target_pairs={{0,2},{1,3},{2,4},{3,5},{4,6},{5,7},{6,8},{7,9},{8,10},{9,11},{10,... | collective-permute-start | bytes 737288 | tf_op jit(solution)/shard_map/ppermute | solution.py:293
  32.9 8.5 %collective-permute-done.15 = bf16[240,512]{1,0:T(8,128)(2,1)S(1)} collective-permute-done((bf16[240,512]{1,0:T(8,128)(2,1)S(1)}, bf16[240,512]{1,0:T(8,128)(2,1)S(1)}, u32[]{:S(2)}, u32[]{:S(2)}) %collective-permute-start.15) | collective-permute-done | bytes 245792 | tf_op jit(solution)/shard_map/ppermute | solution.py:294
  42.0 1.9 %collective-permute-start.17 = (bf16[240,512]{1,0:T(8,128)(2,1)S(1)}, bf16[240,512]{1,0:T(8,128)(2,1)S(1)}, u32[]{:S(2)}, u32[]{:S(2)}) collective-permute-start(bf16[240,512]{1,0:T(8,128)(2,1)S(1)} %add_convert_fusion.3), channel_id=1, source_target_pairs={{0,14},{1,15},{2,0},{3,1},{4,2},{5,3},{6,4},{7,5},{8,6},{9,7},{10,... | collective-permute-start | bytes 737288 | tf_op jit(solution)/shard_map/ppermute | solution.py:294
  46.0 4.6 %collective-permute-done.16 = bf16[240,512]{1,0:T(8,128)(2,1)S(1)} collective-permute-done((bf16[240,512]{1,0:T(8,128)(2,1)S(1)}, bf16[240,512]{1,0:T(8,128)(2,1)S(1)}, u32[]{:S(2)}, u32[]{:S(2)}) %collective-permute-start.16) | collective-permute-done | bytes 245792 | tf_op jit(solution)/shard_map/ppermute | solution.py:293
  50.6 1.4 %collective-permute-done.17 = bf16[240,512]{1,0:T(8,128)(2,1)S(1)} collective-permute-done((bf16[240,512]{1,0:T(8,128)(2,1)S(1)}, bf16[240,512]{1,0:T(8,128)(2,1)S(1)}, u32[]{:S(2)}, u32[]{:S(2)}) %collective-permute-start.17) | collective-permute-done | bytes 245792 | tf_op jit(solution)/shard_map/ppermute | solution.py:294
  52.2 2.0 %collective-permute-start.19 = (bf16[240,512]{1,0:T(8,128)(2,1)S(1)}, bf16[240,512]{1,0:T(8,128)(2,1)S(1)}, u32[]{:S(2)}, u32[]{:S(2)}) collective-permute-start(bf16[240,512]{1,0:T(8,128)(2,1)S(1)} %add_convert_fusion.1), channel_id=1, source_target_pairs={{0,14},{1,15},{2,0},{3,1},{4,2},{5,3},{6,4},{7,5},{8,6},{9,7},{10,... | collective-permute-start | bytes 737288 | tf_op jit(solution)/shard_map/ppermute | solution.py:294
  54.2 1.6 %collective-permute-done.7 = bf16[240,512]{1,0:T(8,128)(2,1)S(1)} collective-permute-done((bf16[240,512]{1,0:T(8,128)(2,1)S(1)}, bf16[240,512]{1,0:T(8,128)(2,1)S(1)}, u32[]{:S(2)}, u32[]{:S(2)}) %collective-permute-start.7) | collective-permute-done | bytes 245792 | tf_op jit(solution)/shard_map/ppermute | solution.py:293
  55.9 1.4 %collective-permute-done.8 = bf16[240,512]{1,0:T(8,128)(2,1)S(1)} collective-permute-done((bf16[240,512]{1,0:T(8,128)(2,1)S(1)}, bf16[240,512]{1,0:T(8,128)(2,1)S(1)}, u32[]{:S(2)}, u32[]{:S(2)}) %collective-permute-start.8) | collective-permute-done | bytes 245792 | tf_op jit(solution)/shard_map/ppermute | solution.py:294
  57.5 2.0 %collective-permute-start.10 = (bf16[240,512]{1,0:T(8,128)(2,1)S(1)}, bf16[240,512]{1,0:T(8,128)(2,1)S(1)}, u32[]{:S(2)}, u32[]{:S(2)}) collective-permute-start(bf16[240,512]{1,0:T(8,128)(2,1)S(1)} %add_convert_fusion.7), channel_id=1, source_target_pairs={{0,14},{1,15},{2,0},{3,1},{4,2},{5,3},{6,4},{7,5},{8,6},{9,7},{10,... | collective-permute-start | bytes 737288 | tf_op jit(solution)/shard_map/ppermute | solution.py:294
  59.5 1.6 %collective-permute-done.18 = bf16[240,512]{1,0:T(8,128)(2,1)S(1)} collective-permute-done((bf16[240,512]{1,0:T(8,128)(2,1)S(1)}, bf16[240,512]{1,0:T(8,128)(2,1)S(1)}, u32[]{:S(2)}, u32[]{:S(2)}) %collective-permute-start.18) | collective-permute-done | bytes 245792 | tf_op jit(solution)/shard_map/ppermute | solution.py:293
  61.1 1.5 %collective-permute-done.19 = bf16[240,512]{1,0:T(8,128)(2,1)S(1)} collective-permute-done((bf16[240,512]{1,0:T(8,128)(2,1)S(1)}, bf16[240,512]{1,0:T(8,128)(2,1)S(1)}, u32[]{:S(2)}, u32[]{:S(2)}) %collective-permute-start.19) | collective-permute-done | bytes 245792 | tf_op jit(solution)/shard_map/ppermute | solution.py:294
  63.5 2.5 %collective-permute-start.20 = (bf16[240,512]{1,0:T(8,128)(2,1)S(1)}, bf16[240,512]{1,0:T(8,128)(2,1)S(1)}, u32[]{:S(2)}, u32[]{:S(2)}) collective-permute-start(bf16[240,512]{1,0:T(8,128)(2,1)S(1)} %add_convert_fusion), channel_id=1, source_target_pairs={{0,2},{1,3},{2,4},{3,5},{4,6},{5,7},{6,8},{7,9},{8,10},{9,11},{10,... | collective-permute-start | bytes 737288 | tf_op jit(solution)/shard_map/ppermute | solution.py:293
  66.4 1.5 %collective-permute-done.10 = bf16[240,512]{1,0:T(8,128)(2,1)S(1)} collective-permute-done((bf16[240,512]{1,0:T(8,128)(2,1)S(1)}, bf16[240,512]{1,0:T(8,128)(2,1)S(1)}, u32[]{:S(2)}, u32[]{:S(2)}) %collective-permute-start.10) | collective-permute-done | bytes 245792 | tf_op jit(solution)/shard_map/ppermute | solution.py:294
  68.8 2.5 %collective-permute-start.11 = (bf16[240,512]{1,0:T(8,128)(2,1)S(1)}, bf16[240,512]{1,0:T(8,128)(2,1)S(1)}, u32[]{:S(2)}, u32[]{:S(2)}) collective-permute-start(bf16[240,512]{1,0:T(8,128)(2,1)S(1)} %add_convert_fusion.6), channel_id=1, source_target_pairs={{0,2},{1,3},{2,4},{3,5},{4,6},{5,7},{6,8},{7,9},{8,10},{9,11},{10,... | collective-permute-start | bytes 737288 | tf_op jit(solution)/shard_map/ppermute | solution.py:293
  71.3 1.8 %collective-permute-done.23 = bf16[240,512]{1,0:T(8,128)(2,1)S(1)} collective-permute-done((bf16[240,512]{1,0:T(8,128)(2,1)S(1)}, bf16[240,512]{1,0:T(8,128)(2,1)S(1)}, u32[]{:S(2)}, u32[]{:S(2)}) %collective-permute-start.23) | collective-permute-done | bytes 245792 | tf_op jit(solution)/shard_map/ppermute | solution.py:294
  73.9 2.5 %collective-permute-start.26 = (bf16[240,512]{1,0:T(8,128)(2,1)S(1)}, bf16[240,512]{1,0:T(8,128)(2,1)S(1)}, u32[]{:S(2)}, u32[]{:S(2)}) collective-permute-start(bf16[240,512]{1,0:T(8,128)(2,1)S(1)} %collective-permute-done.20), channel_id=1, source_target_pairs={{0,2},{1,3},{2,4},{3,5},{4,6},{5,7},{6,8},{7,9},{8,10},{9,11},{10,... | collective-permute-start | bytes 737288 | tf_op jit(solution)/shard_map/ppermute | solution.py:293
  76.4 2.0 %collective-permute-done.21 = bf16[240,512]{1,0:T(8,128)(2,1)S(1)} collective-permute-done((bf16[240,512]{1,0:T(8,128)(2,1)S(1)}, bf16[240,512]{1,0:T(8,128)(2,1)S(1)}, u32[]{:S(2)}, u32[]{:S(2)}) %collective-permute-start.21) | collective-permute-done | bytes 245792 | tf_op jit(solution)/shard_map/ppermute | solution.py:294
  79.2 2.5 %collective-permute-start.25 = (bf16[240,512]{1,0:T(8,128)(2,1)S(1)}, bf16[240,512]{1,0:T(8,128)(2,1)S(1)}, u32[]{:S(2)}, u32[]{:S(2)}) collective-permute-start(bf16[240,512]{1,0:T(8,128)(2,1)S(1)} %collective-permute-done.11), channel_id=1, source_target_pairs={{0,2},{1,3},{2,4},{3,5},{4,6},{5,7},{6,8},{7,9},{8,10},{9,11},{10,... | collective-permute-start | bytes 737288 | tf_op jit(solution)/shard_map/ppermute | solution.py:293
  82.4 3.5 %collective-permute-done.22 = bf16[240,512]{1,0:T(8,128)(2,1)S(1)} collective-permute-done((bf16[240,512]{1,0:T(8,128)(2,1)S(1)}, bf16[240,512]{1,0:T(8,128)(2,1)S(1)}, u32[]{:S(2)}, u32[]{:S(2)}) %collective-permute-start.22) | collective-permute-done | bytes 245792 | tf_op jit(solution)/shard_map/ppermute | solution.py:294
  89.2 25.1 %all_to_all.6 = bf16[16,272,128]{2,1,0:T(8,128)(2,1)S(1)} all-to-all(bf16[16,272,128]{2,1,0:T(8,128)(2,1)S(1)} %shard_map.92), channel_id=1, replica_groups=mesh['aux'=16,'orb'=16] {'aux'}, dimensions={0} | all-to-all | bytes 2228224 | tf_op jit(solution)/shard_map/all_to_all | solution.py:355
  115.8 5.8 %collective-permute-start.30 = (bf16[544,128]{1,0:T(8,128)(2,1)S(1)}, bf16[544,128]{1,0:T(8,128)(2,1)S(1)}, u32[]{:S(2)}, u32[]{:S(2)}) collective-permute-start(bf16[544,128]{1,0:T(8,128)(2,1)S(1)} %pad_maximum_fusion.5), channel_id=1, source_target_pairs={{0,2},{1,32},{16,3},{17,48},{32,18},{33,33},{48,19},{49,49},{64,22... | collective-permute-start | bytes 417800 | tf_op jit(solution)/shard_map/ppermute | solution.py:359
  121.6 8.1 %collective-permute-done.30.both_ref = bf16[544,128]{1,0:T(8,128)(2,1)S(1)} collective-permute-done((bf16[544,128]{1,0:T(8,128)(2,1)S(1)}, bf16[544,128]{1,0:T(8,128)(2,1)S(1)}, u32[]{:S(2)}, u32[]{:S(2)}) %collective-permute-start.30) | collective-permute-done | bytes 139296 | tf_op jit(solution)/shard_map/ppermute | solution.py:359
  129.7 1.8 %shard_map.93 = (bf16[2,128,2,128]{3,2,1,0:T(2,128)(2,1)}, f32[2,2]{1,0:T(2,128)}) custom-call(s32[16,16]{1,0:T(8,128)S(1)} %copy-done.5, s32[32]{0:T(128)S(1)} %copy-done.3, f32[32]{0:T(128)S(1)} %copy-done.7, s32[2,2]{1,0:T(2,128)S(1)} %copy-done.6, bf16[544,128]{1,0:T(8,128)(2,1)S(1)} %collective-permute-done.30.both_ref, f32[16,128]{1,0:T(8,128)S(1)} %bitcast.41), custom_call_target="tpu_custom_call" | custom-call | tf_op jit(solution)/shard_map/pallas_call | solution.py:236
  (93 shorter events, 17.3 us)
Async XLA Ops:
  7.0 7.9 %collective-permute-start.2 = (bf16[1,480,512]{2,1,0:T(8,128)(2,1)S(1)}, bf16[1,480,512]{2,1,0:T(8,128)(2,1)S(1)}, u32[]{:S(2)}, u32[]{:S(2)}) collective-permute-start(bf16[1,480,512]{2,1,0:T(8,128)(2,1)S(1)} %get-tuple-element.44), channel_id=1, source_target_pairs={{0,1},{1,0},{2,3},{3,2},{4,5},{5,4},{6,7},{7,6},{8,9},{9,8},{10,11... | collective-permute-start | bytes 1474568 | tf_op jit(solution)/shard_map/ppermute | solution.py:292
  9.3 12.2 %collective-permute-start.1 = (bf16[2,480,512]{2,1,0:T(8,128)(2,1)S(1)}, bf16[2,480,512]{2,1,0:T(8,128)(2,1)S(1)}, u32[]{:S(2)}, u32[]{:S(2)}) collective-permute-start(bf16[2,480,512]{2,1,0:T(8,128)(2,1)S(1)} %get-tuple-element.46), channel_id=1, source_target_pairs={{0,1},{1,0},{2,3},{3,2},{4,5},{5,4},{6,7},{7,6},{8,9},{9,8},{10,11... | collective-permute-start | bytes 2949128 | tf_op jit(solution)/shard_map/ppermute | solution.py:292
  14.7 17.3 %collective-permute-start = (bf16[5,480,512]{2,1,0:T(8,128)(2,1)S(1)}, bf16[5,480,512]{2,1,0:T(8,128)(2,1)S(1)}, u32[]{:S(2)}, u32[]{:S(2)}) collective-permute-start(bf16[5,480,512]{2,1,0:T(8,128)(2,1)S(1)} %get-tuple-element.49), channel_id=1, source_target_pairs={{0,1},{1,0},{2,3},{3,2},{4,5},{5,4},{6,7},{7,6},{8,9},{9,8},{10,11... | collective-permute-start | bytes 7372808 | tf_op jit(solution)/shard_map/ppermute | solution.py:292
  15.0 12.6 %collective-permute-start.3 = (bf16[120,512]{1,0:T(8,128)(2,1)S(1)}, bf16[120,512]{1,0:T(8,128)(2,1)S(1)}, u32[]{:S(2)}, u32[]{:S(2)}) collective-permute-start(bf16[120,512]{1,0:T(8,128)(2,1)S(1)} %get-tuple-element.56), channel_id=1, source_target_pairs={{0,2},{1,3},{2,4},{3,5},{4,6},{5,7},{6,8},{7,9},{8,10},{9,11},{10,... | collective-permute-start | bytes 368648 | tf_op jit(solution)/shard_map/ppermute | solution.py:293
  18.3 9.6 %collective-permute-start.4 = (bf16[120,512]{1,0:T(8,128)(2,1)S(1)}, bf16[120,512]{1,0:T(8,128)(2,1)S(1)}, u32[]{:S(2)}, u32[]{:S(2)}) collective-permute-start(bf16[120,512]{1,0:T(8,128)(2,1)S(1)} %get-tuple-element.58), channel_id=1, source_target_pairs={{0,14},{1,15},{2,0},{3,1},{4,2},{5,3},{6,4},{7,5},{8,6},{9,7},{10,... | collective-permute-start | bytes 368648 | tf_op jit(solution)/shard_map/ppermute | solution.py:294
  18.3 5.9 %collective-permute-start.12 = (bf16[120,512]{1,0:T(8,128)(2,1)S(1)}, bf16[120,512]{1,0:T(8,128)(2,1)S(1)}, u32[]{:S(2)}, u32[]{:S(2)}) collective-permute-start(bf16[120,512]{1,0:T(8,128)(2,1)S(1)} %get-tuple-element.71), channel_id=1, source_target_pairs={{0,2},{1,3},{2,4},{3,5},{4,6},{5,7},{6,8},{7,9},{8,10},{9,11},{10,... | collective-permute-start | bytes 368648 | tf_op jit(solution)/shard_map/ppermute | solution.py:293
  21.5 6.1 %collective-permute-start.13 = (bf16[120,512]{1,0:T(8,128)(2,1)S(1)}, bf16[120,512]{1,0:T(8,128)(2,1)S(1)}, u32[]{:S(2)}, u32[]{:S(2)}) collective-permute-start(bf16[120,512]{1,0:T(8,128)(2,1)S(1)} %get-tuple-element.73), channel_id=1, source_target_pairs={{0,14},{1,15},{2,0},{3,1},{4,2},{5,3},{6,4},{7,5},{8,6},{9,7},{10,... | collective-permute-start | bytes 368648 | tf_op jit(solution)/shard_map/ppermute | solution.py:294
  27.9 14.0 %collective-permute-start.5 = (bf16[240,512]{1,0:T(8,128)(2,1)S(1)}, bf16[240,512]{1,0:T(8,128)(2,1)S(1)}, u32[]{:S(2)}, u32[]{:S(2)}) collective-permute-start(bf16[240,512]{1,0:T(8,128)(2,1)S(1)} %pad_maximum_fusion.1), channel_id=1, source_target_pairs={{0,2},{1,3},{2,4},{3,5},{4,6},{5,7},{6,8},{7,9},{8,10},{9,11},{10,... | collective-permute-start | bytes 737288 | tf_op jit(solution)/shard_map/ppermute | solution.py:293
  28.3 13.6 %collective-permute-start.6 = (bf16[240,512]{1,0:T(8,128)(2,1)S(1)}, bf16[240,512]{1,0:T(8,128)(2,1)S(1)}, u32[]{:S(2)}, u32[]{:S(2)}) collective-permute-start(bf16[240,512]{1,0:T(8,128)(2,1)S(1)} %pad_maximum_fusion.2), channel_id=1, source_target_pairs={{0,14},{1,15},{2,0},{3,1},{4,2},{5,3},{6,4},{7,5},{8,6},{9,7},{10,... | collective-permute-start | bytes 737288 | tf_op jit(solution)/shard_map/ppermute | solution.py:294
  30.0 11.5 %collective-permute-start.14 = (bf16[240,512]{1,0:T(8,128)(2,1)S(1)}, bf16[240,512]{1,0:T(8,128)(2,1)S(1)}, u32[]{:S(2)}, u32[]{:S(2)}) collective-permute-start(bf16[240,512]{1,0:T(8,128)(2,1)S(1)} %pad_maximum_fusion.3), channel_id=1, source_target_pairs={{0,2},{1,3},{2,4},{3,5},{4,6},{5,7},{6,8},{7,9},{8,10},{9,11},{10,... | collective-permute-start | bytes 737288 | tf_op jit(solution)/shard_map/ppermute | solution.py:293
  31.5 9.9 %collective-permute-start.15 = (bf16[240,512]{1,0:T(8,128)(2,1)S(1)}, bf16[240,512]{1,0:T(8,128)(2,1)S(1)}, u32[]{:S(2)}, u32[]{:S(2)}) collective-permute-start(bf16[240,512]{1,0:T(8,128)(2,1)S(1)} %pad_maximum_fusion.4), channel_id=1, source_target_pairs={{0,14},{1,15},{2,0},{3,1},{4,2},{5,3},{6,4},{7,5},{8,6},{9,7},{10,... | collective-permute-start | bytes 737288 | tf_op jit(solution)/shard_map/ppermute | solution.py:294
  41.6 9.0 %collective-permute-start.16 = (bf16[240,512]{1,0:T(8,128)(2,1)S(1)}, bf16[240,512]{1,0:T(8,128)(2,1)S(1)}, u32[]{:S(2)}, u32[]{:S(2)}) collective-permute-start(bf16[240,512]{1,0:T(8,128)(2,1)S(1)} %add_convert_fusion.4), channel_id=1, source_target_pairs={{0,2},{1,3},{2,4},{3,5},{4,6},{5,7},{6,8},{7,9},{8,10},{9,11},{10,... | collective-permute-start | bytes 737288 | tf_op jit(solution)/shard_map/ppermute | solution.py:293
  42.0 10.0 %collective-permute-start.17 = (bf16[240,512]{1,0:T(8,128)(2,1)S(1)}, bf16[240,512]{1,0:T(8,128)(2,1)S(1)}, u32[]{:S(2)}, u32[]{:S(2)}) collective-permute-start(bf16[240,512]{1,0:T(8,128)(2,1)S(1)} %add_convert_fusion.3), channel_id=1, source_target_pairs={{0,14},{1,15},{2,0},{3,1},{4,2},{5,3},{6,4},{7,5},{8,6},{9,7},{10,... | collective-permute-start | bytes 737288 | tf_op jit(solution)/shard_map/ppermute | solution.py:294
  43.9 11.9 %collective-permute-start.7 = (bf16[240,512]{1,0:T(8,128)(2,1)S(1)}, bf16[240,512]{1,0:T(8,128)(2,1)S(1)}, u32[]{:S(2)}, u32[]{:S(2)}) collective-permute-start(bf16[240,512]{1,0:T(8,128)(2,1)S(1)} %add_convert_fusion.10), channel_id=1, source_target_pairs={{0,2},{1,3},{2,4},{3,5},{4,6},{5,7},{6,8},{7,9},{8,10},{9,11},{10,... | collective-permute-start | bytes 737288 | tf_op jit(solution)/shard_map/ppermute | solution.py:293
  45.3 12.0 %collective-permute-start.8 = (bf16[240,512]{1,0:T(8,128)(2,1)S(1)}, bf16[240,512]{1,0:T(8,128)(2,1)S(1)}, u32[]{:S(2)}, u32[]{:S(2)}) collective-permute-start(bf16[240,512]{1,0:T(8,128)(2,1)S(1)} %add_convert_fusion.9), channel_id=1, source_target_pairs={{0,14},{1,15},{2,0},{3,1},{4,2},{5,3},{6,4},{7,5},{8,6},{9,7},{10,... | collective-permute-start | bytes 737288 | tf_op jit(solution)/shard_map/ppermute | solution.py:294
  52.1 9.0 %collective-permute-start.18 = (bf16[240,512]{1,0:T(8,128)(2,1)S(1)}, bf16[240,512]{1,0:T(8,128)(2,1)S(1)}, u32[]{:S(2)}, u32[]{:S(2)}) collective-permute-start(bf16[240,512]{1,0:T(8,128)(2,1)S(1)} %add_convert_fusion.2), channel_id=1, source_target_pairs={{0,2},{1,3},{2,4},{3,5},{4,6},{5,7},{6,8},{7,9},{8,10},{9,11},{10,... | collective-permute-start | bytes 737288 | tf_op jit(solution)/shard_map/ppermute | solution.py:293
  52.2 10.4 %collective-permute-start.19 = (bf16[240,512]{1,0:T(8,128)(2,1)S(1)}, bf16[240,512]{1,0:T(8,128)(2,1)S(1)}, u32[]{:S(2)}, u32[]{:S(2)}) collective-permute-start(bf16[240,512]{1,0:T(8,128)(2,1)S(1)} %add_convert_fusion.1), channel_id=1, source_target_pairs={{0,14},{1,15},{2,0},{3,1},{4,2},{5,3},{6,4},{7,5},{8,6},{9,7},{10,... | collective-permute-start | bytes 737288 | tf_op jit(solution)/shard_map/ppermute | solution.py:294
  57.4 9.0 %collective-permute-start.9 = (bf16[240,512]{1,0:T(8,128)(2,1)S(1)}, bf16[240,512]{1,0:T(8,128)(2,1)S(1)}, u32[]{:S(2)}, u32[]{:S(2)}) collective-permute-start(bf16[240,512]{1,0:T(8,128)(2,1)S(1)} %add_convert_fusion.8), channel_id=1, source_target_pairs={{0,2},{1,3},{2,4},{3,5},{4,6},{5,7},{6,8},{7,9},{8,10},{9,11},{10,... | collective-permute-start | bytes 737288 | tf_op jit(solution)/shard_map/ppermute | solution.py:293
  57.5 10.4 %collective-permute-start.10 = (bf16[240,512]{1,0:T(8,128)(2,1)S(1)}, bf16[240,512]{1,0:T(8,128)(2,1)S(1)}, u32[]{:S(2)}, u32[]{:S(2)}) collective-permute-start(bf16[240,512]{1,0:T(8,128)(2,1)S(1)} %add_convert_fusion.7), channel_id=1, source_target_pairs={{0,14},{1,15},{2,0},{3,1},{4,2},{5,3},{6,4},{7,5},{8,6},{9,7},{10,... | collective-permute-start | bytes 737288 | tf_op jit(solution)/shard_map/ppermute | solution.py:294
  62.7 10.4 %collective-permute-start.23 = (bf16[240,512]{1,0:T(8,128)(2,1)S(1)}, bf16[240,512]{1,0:T(8,128)(2,1)S(1)}, u32[]{:S(2)}, u32[]{:S(2)}) collective-permute-start(bf16[240,512]{1,0:T(8,128)(2,1)S(1)} %add_convert_fusion), channel_id=1, source_target_pairs={{0,14},{1,15},{2,0},{3,1},{4,2},{5,3},{6,4},{7,5},{8,6},{9,7},{10,... | collective-permute-start | bytes 737288 | tf_op jit(solution)/shard_map/ppermute | solution.py:294
  63.5 9.6 %collective-permute-start.20 = (bf16[240,512]{1,0:T(8,128)(2,1)S(1)}, bf16[240,512]{1,0:T(8,128)(2,1)S(1)}, u32[]{:S(2)}, u32[]{:S(2)}) collective-permute-start(bf16[240,512]{1,0:T(8,128)(2,1)S(1)} %add_convert_fusion), channel_id=1, source_target_pairs={{0,2},{1,3},{2,4},{3,5},{4,6},{5,7},{6,8},{7,9},{8,10},{9,11},{10,... | collective-permute-start | bytes 737288 | tf_op jit(solution)/shard_map/ppermute | solution.py:293
  68.0 10.4 %collective-permute-start.21 = (bf16[240,512]{1,0:T(8,128)(2,1)S(1)}, bf16[240,512]{1,0:T(8,128)(2,1)S(1)}, u32[]{:S(2)}, u32[]{:S(2)}) collective-permute-start(bf16[240,512]{1,0:T(8,128)(2,1)S(1)} %add_convert_fusion.6), channel_id=1, source_target_pairs={{0,14},{1,15},{2,0},{3,1},{4,2},{5,3},{6,4},{7,5},{8,6},{9,7},{10,... | collective-permute-start | bytes 737288 | tf_op jit(solution)/shard_map/ppermute | solution.py:294
  68.8 9.6 %collective-permute-start.11 = (bf16[240,512]{1,0:T(8,128)(2,1)S(1)}, bf16[240,512]{1,0:T(8,128)(2,1)S(1)}, u32[]{:S(2)}, u32[]{:S(2)}) collective-permute-start(bf16[240,512]{1,0:T(8,128)(2,1)S(1)} %add_convert_fusion.6), channel_id=1, source_target_pairs={{0,2},{1,3},{2,4},{3,5},{4,6},{5,7},{6,8},{7,9},{8,10},{9,11},{10,... | collective-permute-start | bytes 737288 | tf_op jit(solution)/shard_map/ppermute | solution.py:293
  73.1 12.9 %collective-permute-start.24 = (bf16[240,512]{1,0:T(8,128)(2,1)S(1)}, bf16[240,512]{1,0:T(8,128)(2,1)S(1)}, u32[]{:S(2)}, u32[]{:S(2)}) collective-permute-start(bf16[240,512]{1,0:T(8,128)(2,1)S(1)} %collective-permute-done.23), channel_id=1, source_target_pairs={{0,14},{1,15},{2,0},{3,1},{4,2},{5,3},{6,4},{7,5},{8,6},{9,7},{10,... | collective-permute-start | bytes 737288 | tf_op jit(solution)/shard_map/ppermute | solution.py:294
  73.9 12.1 %collective-permute-start.26 = (bf16[240,512]{1,0:T(8,128)(2,1)S(1)}, bf16[240,512]{1,0:T(8,128)(2,1)S(1)}, u32[]{:S(2)}, u32[]{:S(2)}) collective-permute-start(bf16[240,512]{1,0:T(8,128)(2,1)S(1)} %collective-permute-done.20), channel_id=1, source_target_pairs={{0,2},{1,3},{2,4},{3,5},{4,6},{5,7},{6,8},{7,9},{8,10},{9,11},{10,... | collective-permute-start | bytes 737288 | tf_op jit(solution)/shard_map/ppermute | solution.py:293
  78.4 7.6 %collective-permute-start.22 = (bf16[240,512]{1,0:T(8,128)(2,1)S(1)}, bf16[240,512]{1,0:T(8,128)(2,1)S(1)}, u32[]{:S(2)}, u32[]{:S(2)}) collective-permute-start(bf16[240,512]{1,0:T(8,128)(2,1)S(1)} %collective-permute-done.21), channel_id=1, source_target_pairs={{0,14},{1,15},{2,0},{3,1},{4,2},{5,3},{6,4},{7,5},{8,6},{9,7},{10,... | collective-permute-start | bytes 737288 | tf_op jit(solution)/shard_map/ppermute | solution.py:294
  79.2 6.8 %collective-permute-start.25 = (bf16[240,512]{1,0:T(8,128)(2,1)S(1)}, bf16[240,512]{1,0:T(8,128)(2,1)S(1)}, u32[]{:S(2)}, u32[]{:S(2)}) collective-permute-start(bf16[240,512]{1,0:T(8,128)(2,1)S(1)} %collective-permute-done.11), channel_id=1, source_target_pairs={{0,2},{1,3},{2,4},{3,5},{4,6},{5,7},{6,8},{7,9},{8,10},{9,11},{10,... | collective-permute-start | bytes 737288 | tf_op jit(solution)/shard_map/ppermute | solution.py:293
  82.3 4.4 %collective-permute-start.27 = (bf16[10,272,128]{2,1,0:T(8,128)(2,1)S(1)}, bf16[10,272,128]{2,1,0:T(8,128)(2,1)S(1)}, u32[]{:S(2)}, u32[]{:S(2)}) collective-permute-start(bf16[10,272,128]{2,1,0:T(8,128)(2,1)S(1)} %shard_map.89), channel_id=1, source_target_pairs={{0,1},{1,0},{2,3},{3,2},{4,5},{5,4},{6,7},{7,6},{8,9},{9,8},{10,11... | collective-permute-start | bytes 2088968 | tf_op jit(solution)/shard_map/ppermute | solution.py:292
  86.7 1.8 %collective-permute-start.28 = (bf16[6,272,128]{2,1,0:T(8,128)(2,1)S(1)}, bf16[6,272,128]{2,1,0:T(8,128)(2,1)S(1)}, u32[]{:S(2)}, u32[]{:S(2)}) collective-permute-start(bf16[6,272,128]{2,1,0:T(8,128)(2,1)S(1)} %shard_map.91), channel_id=1, source_target_pairs={{0,1},{1,0},{2,3},{3,2},{4,5},{5,4},{6,7},{7,6},{8,9},{9,8},{10,11... | collective-permute-start | bytes 1253384 | tf_op jit(solution)/shard_map/ppermute | solution.py:292
  89.1 40.6 %copy-start.3 = (s32[32]{0:T(128)S(1)}, s32[32]{0:T(128)}, u32[]{:S(2)}) copy-start(s32[32]{0:T(128)} %domains.7) | copy-start | bytes 388
  114.5 1.3 %collective-permute-start.29 = (bf16[272,128]{1,0:T(8,128)(2,1)S(1)}, bf16[272,128]{1,0:T(8,128)(2,1)S(1)}, u32[]{:S(2)}, u32[]{:S(2)}) collective-permute-start(bf16[272,128]{1,0:T(8,128)(2,1)S(1)} %reduce_sum.12), channel_id=1, source_target_pairs={{0,1},{1,0},{2,3},{3,2},{4,5},{5,4},{6,7},{7,6},{8,9},{9,8},{10,11... | collective-permute-start | bytes 208904 | tf_op jit(solution)/shard_map/ppermute | solution.py:292
  115.8 13.9 %collective-permute-start.30 = (bf16[544,128]{1,0:T(8,128)(2,1)S(1)}, bf16[544,128]{1,0:T(8,128)(2,1)S(1)}, u32[]{:S(2)}, u32[]{:S(2)}) collective-permute-start(bf16[544,128]{1,0:T(8,128)(2,1)S(1)} %pad_maximum_fusion.5), channel_id=1, source_target_pairs={{0,2},{1,32},{16,3},{17,48},{32,18},{33,33},{48,19},{49,49},{64,22... | collective-permute-start | bytes 417800 | tf_op jit(solution)/shard_map/ppermute | solution.py:359
  (7 other events, 167.1 us)

commit v3 on v2

--- a/solution.py
+++ b/solution.py
@@ -17,67 +17,69 @@
 EARLY = 10
 SLOTS = 16
 RINGS = 2
-TRANSFORM_VMEM = 24 * 2**20
+TRANSFORM_VMEM = 57 * 2**20
+GROUPS = (1, 2, 5)
 PAIR_VMEM = 32 * 2**20
 
 
-def transform_rows(out_ref, rows, a_at, coeff_at):
-    for q in range(OWN):
-        out_ref[:, q * BS : (q + 1) * BS] = jnp.dot(
-            a_at(q, rows), coeff_at(q), preferred_element_type=jnp.float32
-        ).astype(out_ref.dtype)
-
-
-def core_halves():
-    core = lax.axis_index("orb") % 2
-    return 1 - core, core
-
-
-def transform_kernel(firsts, domains, a_hbm, c_hbm, send_ref, own_ref, a_ref, c_ref, sems):
-    copies = []
-    for n, first in enumerate(firsts):
-        chunk = (lax.axis_index("orb") // 2 + first) % CHIPS
-        here = []
-        for q in range(OWN):
-            lanes = pl.ds(pl.multiple_of(domains[OWN * chunk + q] * BS, BS), BS)
-            here.append((c_hbm.at[:, lanes], c_ref.at[n, q]))
-        for side, half in enumerate(core_halves()):
-            here.append((a_hbm.at[pl.ds(OWN * chunk, OWN), half], a_ref.at[n, side]))
-        copies.append(
-            [pltpu.make_async_copy(x, y, sems.at[n, k]) for k, (x, y) in enumerate(here)]
-        )
-        for copy in copies[-1]:
-            copy.start()
-    for n in range(len(firsts)):
-        for copy in copies[n][:-1]:
-            copy.wait()
-        transform_rows(send_ref.at[n], 0, lambda q, side: a_ref[n, side, q], lambda q: c_ref[n, q])
-        copies[n][-1].wait()
-        transform_rows(own_ref.at[n], 1, lambda q, side: a_ref[n, side, q], lambda q: c_ref[n, q])
-
-
-def transform_call(domains, integrals, coeffs, firsts):
-    half, width, count = integrals.shape[2], OWN * BS, len(firsts)
+def transform_kernel(order, domains, a_hbm, c_hbm, *refs):
+    outs, (a_ref, c_ref, out_ref, sems, out_sems) = refs[:-5], refs[-5:]
+    chip, core = lax.axis_index("orb") // 2, lax.axis_index("orb") % 2
+    chunks = [(chip + distance) % CHIPS for distance in order]
+    places = [(g, n) for g, count in enumerate(GROUPS) for n in range(count)]
+    copies = [pltpu.make_async_copy(c_hbm, c_ref, sems.at[len(order)])]
+    copies += [
+        pltpu.make_async_copy(a_hbm.at[pl.ds(OWN * chunk, OWN)], a_ref.at[n], sems.at[n])
+        for n, chunk in enumerate(chunks)
+    ]
+    for copy in copies:
+        copy.start()
+    copies[0].wait()
+    zeros = jnp.zeros((BS, BS), jnp.bfloat16)
+    results = []
+    for n, chunk in enumerate(chunks):
+        copies[1 + n].wait()
+        group, index = places[n]
+        for q in range(0, OWN, 2):
+            c0, c1 = (
+                c_ref[:, pl.ds(pl.multiple_of(domains[OWN * chunk + q + k] * BS, BS), BS)]
+                for k in range(2)
+            )
+            chosen = jnp.concatenate(
+                [jnp.concatenate([c0, zeros], 1), jnp.concatenate([zeros, c1], 1)], 0
+            )
+            for side, half in enumerate((1 - core, core)):
+                left = jnp.concatenate([a_ref[n, q, half], a_ref[n, q + 1, half]], 1)
+                out_ref[n, side, :, q * BS : (q + 2) * BS] = jnp.dot(
+                    left, chosen, preferred_element_type=jnp.float32
+                ).astype(jnp.bfloat16)
+        for side in range(2):
+            results.append(
+                pltpu.make_async_copy(
+                    out_ref.at[n, side], outs[2 * group + side].at[index], out_sems.at[n, side]
+                )
+            )
+            results[-1].start()
+    for result in results:
+        result.wait()
+
+
+def transform_call(domains, integrals, coeffs, order):
+    half, width, count = integrals.shape[2], OWN * BS, len(order)
     hbm = pl.BlockSpec(memory_space=pltpu.HBM)
-    vmem = pl.BlockSpec(memory_space=pltpu.VMEM)
+    outs = [jax.ShapeDtypeStruct((n, half, width), jnp.bfloat16) for n in GROUPS for _ in range(2)]
     return pl.pallas_call(
-        functools.partial(transform_kernel, firsts),
+        functools.partial(transform_kernel, order),
         in_specs=[pl.BlockSpec(memory_space=pltpu.SMEM), hbm, hbm],
-        out_specs=(vmem, vmem),
+        out_specs=(hbm,) * len(outs),
         scratch_shapes=[
-            pltpu.VMEM((count, 2, OWN, half, BS), jnp.bfloat16),
-            pltpu.VMEM((count, OWN, BS, BS), jnp.bfloat16),
-            pltpu.SemaphoreType.DMA((count, OWN + 2)),
+            pltpu.VMEM((count, OWN, 2, half, BS), jnp.bfloat16),
+            pltpu.VMEM(coeffs.shape, jnp.bfloat16),
+            pltpu.VMEM((count, 2, half, width), jnp.bfloat16),
+            pltpu.SemaphoreType.DMA((count + 1,)),
+            pltpu.SemaphoreType.DMA((count, 2)),
         ],
-        out_shape=(
-            jax.ShapeDtypeStruct((count, half, width), jnp.bfloat16),
-            jax.ShapeDtypeStruct((count, half, width), jnp.float32),
-        ),
-        cost_estimate=pl.CostEstimate(
-            flops=4 * count * half * width * BS,
-            bytes_accessed=count * half * (4 * width + 6 * width),
-            transcendentals=0,
-        ),
+        out_shape=tuple(outs),
         compiler_params=pltpu.CompilerParams(vmem_limit_bytes=TRANSFORM_VMEM),
     )(domains, integrals, coeffs)
 
@@ -294,30 +296,30 @@
     down = lambda x: lax.ppermute(x, "orb", [(o, (o - 2) % n_orb) for o in range(n_orb)])
 
     part = half // RINGS
-    terms = {}
-
-    def after(x, *others):
-        return tie((x, *others))[0]
-
-    def transform(firsts, *others):
-        send, mine = transform_call(domains, after(integrals, *others), coeffs, firsts)
-        theirs = swap(send)
-        values = [
-            mine[n, first : first + part] + theirs[n, first : first + part].astype(f32)
-            for n in range(len(firsts))
-            for first in range(0, half, part)
-        ]
-        if len(firsts) > 1:
-            values = tie(values)
-        terms.update({k: values[RINGS * n : RINGS * (n + 1)] for n, k in enumerate(firsts)})
-        return send
-
     def add(x, *received):
         return sum((r.astype(f32) for r in received), x).astype(jnp.bfloat16)
 
-    send = transform((4,))
-    send = transform((3, 5), send)
-    transform((2, 6, 1, 7, 0), send)
+    order = (4, 3, 5, 2, 6, 1, 7, 0)
+    outs = transform_call(domains, integrals, coeffs, order)
+    rows = [slice(first, first + part) for first in range(0, half, part)]
+    terms, begin, first_theirs = {}, 0, None
+    for group, count in enumerate(GROUPS):
+        send, mine = outs[2 * group : 2 * group + 2]
+        if first_theirs is None:
+            theirs = first_theirs = swap(send)
+        else:
+            theirs = swap(tie((send, first_theirs))[0])
+        values = tie(
+            [
+                mine[n, r].astype(f32) + theirs[n, r].astype(f32)
+                for n in range(count)
+                for r in rows
+            ]
+        )
+        for n in range(count):
+            terms[order[begin + n]] = values[RINGS * n : RINGS * (n + 1)]
+        begin += count
+
     h = part // 2
     starts = [tie((add(x[:h]), add(x[h:]))) for x in terms[4]]
     sums = [(up(u), down(d)) for u, d in starts]

time: 133 us -> 130 us (0.977)
  local copies, waits for them, and re-layouts: 5.21 us -> 0.29 us
  starting transfers between devices: 38.9 us -> 41.9 us
  other arithmetic: 2.51 us -> 4.67 us
    ppermute x12, starting transfers between devices: 20 us -> 35.2 us  [shards(): lax.ppermute(x, 'orb', [(o, (o + 2) % n_orb) for o in range(n_orb)])]
    ppermute x12, waiting for transfers between devices: 25 us -> 15.1 us  [shards(): lax.ppermute(x, 'orb', [(o, (o - 2) % n_orb) for o in range(n_orb)])]
    ppermute x12, starting transfers between devices: 12 us -> 3.56 us  [shards(): lax.ppermute(x, 'orb', [(o, (o - 2) % n_orb) for o in range(n_orb)])]
    unnamed x20 -> x16, local copies, waits for them, and re-layouts: 5.02 us -> 0.1 us
    ppermute x1, starting transfers between devices: 5.77 us -> 2.26 us  [shards(): both = lax.ppermute(both, ('aux', 'orb'), pairs)]
    ppermute x1, waiting for transfers between devices: 8.11 us -> 11.6 us  [shards(): both = lax.ppermute(both, ('aux', 'orb'), pairs)]
    ppermute x6, waiting for transfers between devices: 2.39 us -> 5.68 us  [shards(): swap = lambda x: lax.ppermute(x, 'orb', [(o, o ^ 1) for o in range(n_orb)])]
    add x3, other arithmetic: 1.2 us -> 3.55 us  [shards(): mine[n, r].astype(f32) + theirs[n, r].astype(f32)]
  transfers between devices with their start and end apart: 31 -> 31, of which waited for: 17 -> 21; matrix products, arithmetic and copies ran while one was open for 2% -> 4% of each run, Pallas kernels for 7% -> 1%
where the time goes in v3:
time: 130 us; the launch traced here: 129 us
  waiting for transfers between devices  44.8 us (34%)
  starting transfers between devices  41.9 us (32%)
  blocking collectives  25.1 us (19%)
  Pallas kernels  11.5 us (9%)
  other arithmetic  4.67 us (4%)
    ppermute x12, starting transfers between devices, shards(): lax.ppermute(x, 'orb', [(o, (o + 2) % n_orb) for o in range(n_orb)])  35.2 us
    all_to_all x1, blocking collectives, shards(): lax.all_to_all(sums.reshape(SLOTS * ROWS, BS), 'aux', 0, 0, tiled=True)  25.1 us
    ppermute x12, waiting for transfers between devices, shards(): lax.ppermute(x, 'orb', [(o, (o - 2) % n_orb) for o in range(n_orb)])  15.1 us
    ppermute x12, waiting for transfers between devices, shards(): lax.ppermute(x, 'orb', [(o, (o + 2) % n_orb) for o in range(n_orb)])  12.4 us
    ppermute x1, waiting for transfers between devices, shards(): both = lax.ppermute(both, ('aux', 'orb'), pairs)  11.6 us
    pallas_call x1, Pallas kernels, transform_call(): pl.pallas_call(functools.partial(transform_kernel, order), in_specs=[pl.B...  7.32 us
    ppermute x6, waiting for transfers between devices, shards(): swap = lambda x: lax.ppermute(x, 'orb', [(o, o ^ 1) for o in range(n_orb)])  5.68 us
    ppermute x12, starting transfers between devices, shards(): lax.ppermute(x, 'orb', [(o, (o - 2) % n_orb) for o in range(n_orb)])  3.56 us
  transfers between devices with their start and end apart: 31, of which 21 were waited for; matrix products, arithmetic and copies ran while one was open for 4% of the time, Pallas kernels for 1%

profile of v3, /device:TPU:96, one launch (start us, length us, event | category | flops | bytes accessed | tf_op | source)
XLA Modules:
  0.0 129.5 jit_solution(4033688676395879390)
XLA Ops:
  0.6 7.3 %shard_map.86 = (bf16[1,480,512]{2,1,0:T(8,128)(2,1)}, bf16[1,480,512]{2,1,0:T(8,128)(2,1)}, bf16[2,480,512]{2,1,0:T(8,128)(2,1)}, bf16[2,480,512]{2,1,0:T(8,128...) custom-call(s32[32]{0:T(128)} %domains.3, bf16[32,2,480,128]{3,2,1,0:T(8,128)(2,1)} %bitcast.35, ...), custom_call_target="tpu_custom_call" | custom-call | tf_op jit(solution)/shard_map/pallas_call | solution.py:71
  8.1 2.1 %collective-permute-done = bf16[1,480,512]{2,1,0:T(8,128)(2,1)S(1)} collective-permute-done((bf16[1,480,512]{2,1,0:T(8,128)(2,1)}, bf16[1,480,512]{2,1,0:T(8,128)(2,1)S(1)}, u32[]{:S(2)}, u32[]{:S(2)}) %collective-permute-start) | collective-permute-done | bytes 491552 | tf_op jit(solution)/shard_map/ppermute | solution.py:294
  12.1 3.1 %collective-permute-start.12 = (bf16[120,512]{1,0:T(8,128)(2,1)S(1)}, bf16[120,512]{1,0:T(8,128)(2,1)S(1)}, u32[]{:S(2)}, u32[]{:S(2)}) collective-permute-start(bf16[120,512]{1,0:T(8,128)(2,1)S(1)} %get-tuple-element.75), channel_id=1, source_target_pairs={{0,2},{1,3},{2,4},{3,5},{4,6},{5,7},{6,8},{7,9},{8,10},{9,11},{10,... | collective-permute-start | bytes 368648 | tf_op jit(solution)/shard_map/ppermute | solution.py:295
  15.2 1.2 collective-permute-done.2
  16.4 3.1 %collective-permute-start.3 = (bf16[120,512]{1,0:T(8,128)(2,1)S(1)}, bf16[120,512]{1,0:T(8,128)(2,1)S(1)}, u32[]{:S(2)}, u32[]{:S(2)}) collective-permute-start(bf16[120,512]{1,0:T(8,128)(2,1)S(1)} %get-tuple-element.59), channel_id=1, source_target_pairs={{0,2},{1,3},{2,4},{3,5},{4,6},{5,7},{6,8},{7,9},{8,10},{9,11},{10,... | collective-permute-start | bytes 368648 | tf_op jit(solution)/shard_map/ppermute | solution.py:295
  19.6 1.7 %add_bitcast_fusion.2 = (f32[240,512]{1,0:T(8,128)S(1)}, f32[240,512]{1,0:T(8,128)S(1)}, f32[240,512]{1,0:T(8,128)S(1)}, f32[240,512]{1,0:T(8,128)S(1)}, f32[240,512]{1,0:T(8,128)S(1)}) fusion(bf16[2,480,512]{2,1,0:T(8,128)(2,1)S(1)} %collective-permute-done.2, bf16[2,480,512]{2,1,0:T(8,128)(2,1)} %get-tuple-element.53, ...), kind=kLoop, calls=%fused_computation.13 | loop fusion | flops 1843200 | bytes 4915200 | tf_op jit(solution)/shard_map/add | solution.py:314
  22.2 3.3 %collective-permute-start.14 = (bf16[240,512]{1,0:T(8,128)(2,1)S(1)}, bf16[240,512]{1,0:T(8,128)(2,1)S(1)}, u32[]{:S(2)}, u32[]{:S(2)}) collective-permute-start(bf16[240,512]{1,0:T(8,128)(2,1)S(1)} %pad_maximum_fusion.3), channel_id=1, source_target_pairs={{0,2},{1,3},{2,4},{3,5},{4,6},{5,7},{6,8},{7,9},{8,10},{9,11},{10,... | collective-permute-start | bytes 737288 | tf_op jit(solution)/shard_map/ppermute | solution.py:295
  25.8 3.2 %collective-permute-start.5 = (bf16[240,512]{1,0:T(8,128)(2,1)S(1)}, bf16[240,512]{1,0:T(8,128)(2,1)S(1)}, u32[]{:S(2)}, u32[]{:S(2)}) collective-permute-start(bf16[240,512]{1,0:T(8,128)(2,1)S(1)} %pad_maximum_fusion.1), channel_id=1, source_target_pairs={{0,2},{1,3},{2,4},{3,5},{4,6},{5,7},{6,8},{7,9},{8,10},{9,11},{10,... | collective-permute-start | bytes 737288 | tf_op jit(solution)/shard_map/ppermute | solution.py:295
  29.0 2.5 %collective-permute-done.15 = bf16[240,512]{1,0:T(8,128)(2,1)S(1)} collective-permute-done((bf16[240,512]{1,0:T(8,128)(2,1)S(1)}, bf16[240,512]{1,0:T(8,128)(2,1)S(1)}, u32[]{:S(2)}, u32[]{:S(2)}) %collective-permute-start.15) | collective-permute-done | bytes 245792 | tf_op jit(solution)/shard_map/ppermute | solution.py:296
  32.6 3.5 %collective-permute-start.16 = (bf16[240,512]{1,0:T(8,128)(2,1)S(1)}, bf16[240,512]{1,0:T(8,128)(2,1)S(1)}, u32[]{:S(2)}, u32[]{:S(2)}) collective-permute-start(bf16[240,512]{1,0:T(8,128)(2,1)S(1)} %add_convert_fusion.4), channel_id=1, source_target_pairs={{0,2},{1,3},{2,4},{3,5},{4,6},{5,7},{6,8},{7,9},{8,10},{9,11},{10,... | collective-permute-start | bytes 737288 | tf_op jit(solution)/shard_map/ppermute | solution.py:295
  37.3 3.8 %collective-permute-start.7 = (bf16[240,512]{1,0:T(8,128)(2,1)S(1)}, bf16[240,512]{1,0:T(8,128)(2,1)S(1)}, u32[]{:S(2)}, u32[]{:S(2)}) collective-permute-start(bf16[240,512]{1,0:T(8,128)(2,1)S(1)} %add_convert_fusion.9), channel_id=1, source_target_pairs={{0,2},{1,3},{2,4},{3,5},{4,6},{5,7},{6,8},{7,9},{8,10},{9,11},{10,... | collective-permute-start | bytes 737288 | tf_op jit(solution)/shard_map/ppermute | solution.py:295
  41.1 1.6 %collective-permute-done.17 = bf16[240,512]{1,0:T(8,128)(2,1)S(1)} collective-permute-done((bf16[240,512]{1,0:T(8,128)(2,1)S(1)}, bf16[240,512]{1,0:T(8,128)(2,1)S(1)}, u32[]{:S(2)}, u32[]{:S(2)}) %collective-permute-start.17) | collective-permute-done | bytes 245792 | tf_op jit(solution)/shard_map/ppermute | solution.py:296
  42.9 3.4 %collective-permute-start.18 = (bf16[240,512]{1,0:T(8,128)(2,1)S(1)}, bf16[240,512]{1,0:T(8,128)(2,1)S(1)}, u32[]{:S(2)}, u32[]{:S(2)}) collective-permute-start(bf16[240,512]{1,0:T(8,128)(2,1)S(1)} %add_convert_fusion.2), channel_id=1, source_target_pairs={{0,2},{1,3},{2,4},{3,5},{4,6},{5,7},{6,8},{7,9},{8,10},{9,11},{10,... | collective-permute-start | bytes 737288 | tf_op jit(solution)/shard_map/ppermute | solution.py:295
  46.4 1.3 %collective-permute-done.7 = bf16[240,512]{1,0:T(8,128)(2,1)S(1)} collective-permute-done((bf16[240,512]{1,0:T(8,128)(2,1)S(1)}, bf16[240,512]{1,0:T(8,128)(2,1)S(1)}, u32[]{:S(2)}, u32[]{:S(2)}) %collective-permute-start.7) | collective-permute-done | bytes 245792 | tf_op jit(solution)/shard_map/ppermute | solution.py:295
  47.8 1.9 %collective-permute-start.10 = (bf16[240,512]{1,0:T(8,128)(2,1)S(1)}, bf16[240,512]{1,0:T(8,128)(2,1)S(1)}, u32[]{:S(2)}, u32[]{:S(2)}) collective-permute-start(bf16[240,512]{1,0:T(8,128)(2,1)S(1)} %add_convert_fusion.6), channel_id=1, source_target_pairs={{0,14},{1,15},{2,0},{3,1},{4,2},{5,3},{6,4},{7,5},{8,6},{9,7},{10,... | collective-permute-start | bytes 737288 | tf_op jit(solution)/shard_map/ppermute | solution.py:296
  49.6 2.0 %collective-permute-start.9 = (bf16[240,512]{1,0:T(8,128)(2,1)S(1)}, bf16[240,512]{1,0:T(8,128)(2,1)S(1)}, u32[]{:S(2)}, u32[]{:S(2)}) collective-permute-start(bf16[240,512]{1,0:T(8,128)(2,1)S(1)} %add_convert_fusion.7), channel_id=1, source_target_pairs={{0,2},{1,3},{2,4},{3,5},{4,6},{5,7},{6,8},{7,9},{8,10},{9,11},{10,... | collective-permute-start | bytes 737288 | tf_op jit(solution)/shard_map/ppermute | solution.py:295
  51.6 1.3 %collective-permute-done.18 = bf16[240,512]{1,0:T(8,128)(2,1)S(1)} collective-permute-done((bf16[240,512]{1,0:T(8,128)(2,1)S(1)}, bf16[240,512]{1,0:T(8,128)(2,1)S(1)}, u32[]{:S(2)}, u32[]{:S(2)}) %collective-permute-start.18) | collective-permute-done | bytes 245792 | tf_op jit(solution)/shard_map/ppermute | solution.py:295
  53.0 2.0 %collective-permute-done.19 = bf16[240,512]{1,0:T(8,128)(2,1)S(1)} collective-permute-done((bf16[240,512]{1,0:T(8,128)(2,1)S(1)}, bf16[240,512]{1,0:T(8,128)(2,1)S(1)}, u32[]{:S(2)}, u32[]{:S(2)}) %collective-permute-start.19) | collective-permute-done | bytes 245792 | tf_op jit(solution)/shard_map/ppermute | solution.py:296
  55.0 1.8 %collective-permute-start.20 = (bf16[240,512]{1,0:T(8,128)(2,1)S(1)}, bf16[240,512]{1,0:T(8,128)(2,1)S(1)}, u32[]{:S(2)}, u32[]{:S(2)}) collective-permute-start(bf16[240,512]{1,0:T(8,128)(2,1)S(1)} %add_convert_fusion), channel_id=1, source_target_pairs={{0,2},{1,3},{2,4},{3,5},{4,6},{5,7},{6,8},{7,9},{8,10},{9,11},{10,... | collective-permute-start | bytes 737288 | tf_op jit(solution)/shard_map/ppermute | solution.py:295
  58.6 3.5 %collective-permute-start.11 = (bf16[240,512]{1,0:T(8,128)(2,1)S(1)}, bf16[240,512]{1,0:T(8,128)(2,1)S(1)}, u32[]{:S(2)}, u32[]{:S(2)}) collective-permute-start(bf16[240,512]{1,0:T(8,128)(2,1)S(1)} %add_convert_fusion.5), channel_id=1, source_target_pairs={{0,2},{1,3},{2,4},{3,5},{4,6},{5,7},{6,8},{7,9},{8,10},{9,11},{10,... | collective-permute-start | bytes 737288 | tf_op jit(solution)/shard_map/ppermute | solution.py:295
  62.2 1.8 %collective-permute-done.20 = bf16[240,512]{1,0:T(8,128)(2,1)S(1)} collective-permute-done((bf16[240,512]{1,0:T(8,128)(2,1)S(1)}, bf16[240,512]{1,0:T(8,128)(2,1)S(1)}, u32[]{:S(2)}, u32[]{:S(2)}) %collective-permute-start.20) | collective-permute-done | bytes 245792 | tf_op jit(solution)/shard_map/ppermute | solution.py:295
  64.0 1.6 %collective-permute-done.23 = bf16[240,512]{1,0:T(8,128)(2,1)S(1)} collective-permute-done((bf16[240,512]{1,0:T(8,128)(2,1)S(1)}, bf16[240,512]{1,0:T(8,128)(2,1)S(1)}, u32[]{:S(2)}, u32[]{:S(2)}) %collective-permute-start.23) | collective-permute-done | bytes 245792 | tf_op jit(solution)/shard_map/ppermute | solution.py:296
  65.6 1.6 %collective-permute-start.26 = (bf16[240,512]{1,0:T(8,128)(2,1)S(1)}, bf16[240,512]{1,0:T(8,128)(2,1)S(1)}, u32[]{:S(2)}, u32[]{:S(2)}) collective-permute-start(bf16[240,512]{1,0:T(8,128)(2,1)S(1)} %collective-permute-done.20), channel_id=1, source_target_pairs={{0,2},{1,3},{2,4},{3,5},{4,6},{5,7},{6,8},{7,9},{8,10},{9,11},{10,... | collective-permute-start | bytes 737288 | tf_op jit(solution)/shard_map/ppermute | solution.py:295
  67.2 2.1 %collective-permute-done.11 = bf16[240,512]{1,0:T(8,128)(2,1)S(1)} collective-permute-done((bf16[240,512]{1,0:T(8,128)(2,1)S(1)}, bf16[240,512]{1,0:T(8,128)(2,1)S(1)}, u32[]{:S(2)}, u32[]{:S(2)}) %collective-permute-start.11) | collective-permute-done | bytes 245792 | tf_op jit(solution)/shard_map/ppermute | solution.py:295
  69.5 2.9 %collective-permute-start.25 = (bf16[240,512]{1,0:T(8,128)(2,1)S(1)}, bf16[240,512]{1,0:T(8,128)(2,1)S(1)}, u32[]{:S(2)}, u32[]{:S(2)}) collective-permute-start(bf16[240,512]{1,0:T(8,128)(2,1)S(1)} %collective-permute-done.11), channel_id=1, source_target_pairs={{0,2},{1,3},{2,4},{3,5},{4,6},{5,7},{6,8},{7,9},{8,10},{9,11},{10,... | collective-permute-start | bytes 737288 | tf_op jit(solution)/shard_map/ppermute | solution.py:295
  73.6 4.2 %collective-permute-done.25 = bf16[240,512]{1,0:T(8,128)(2,1)S(1)} collective-permute-done((bf16[240,512]{1,0:T(8,128)(2,1)S(1)}, bf16[240,512]{1,0:T(8,128)(2,1)S(1)}, u32[]{:S(2)}, u32[]{:S(2)}) %collective-permute-start.25) | collective-permute-done | bytes 245792 | tf_op jit(solution)/shard_map/ppermute | solution.py:295
  77.9 5.9 %collective-permute-done.22 = bf16[240,512]{1,0:T(8,128)(2,1)S(1)} collective-permute-done((bf16[240,512]{1,0:T(8,128)(2,1)S(1)}, bf16[240,512]{1,0:T(8,128)(2,1)S(1)}, u32[]{:S(2)}, u32[]{:S(2)}) %collective-permute-start.22) | collective-permute-done | bytes 245792 | tf_op jit(solution)/shard_map/ppermute | solution.py:296
  87.0 25.1 %all_to_all.6 = bf16[16,272,128]{2,1,0:T(8,128)(2,1)S(1)} all-to-all(bf16[16,272,128]{2,1,0:T(8,128)(2,1)S(1)} %shard_map.90), channel_id=1, replica_groups=mesh['aux'=16,'orb'=16] {'aux'}, dimensions={0} | all-to-all | bytes 2228224 | tf_op jit(solution)/shard_map/all_to_all | solution.py:357
  112.4 1.2 collective-permute-done.29
  113.6 2.3 %collective-permute-start.30 = (bf16[544,128]{1,0:T(8,128)(2,1)S(1)}, bf16[544,128]{1,0:T(8,128)(2,1)S(1)}, u32[]{:S(2)}, u32[]{:S(2)}) collective-permute-start(bf16[544,128]{1,0:T(8,128)(2,1)S(1)} %pad_maximum_fusion.5), channel_id=1, source_target_pairs={{0,2},{1,32},{16,3},{17,48},{32,18},{33,33},{48,19},{49,49},{64,22... | collective-permute-start | bytes 417800 | tf_op jit(solution)/shard_map/ppermute | solution.py:361
  115.9 11.6 %collective-permute-done.30.both_ref = bf16[544,128]{1,0:T(8,128)(2,1)S(1)} collective-permute-done((bf16[544,128]{1,0:T(8,128)(2,1)S(1)}, bf16[544,128]{1,0:T(8,128)(2,1)S(1)}, u32[]{:S(2)}, u32[]{:S(2)}) %collective-permute-start.30) | collective-permute-done | bytes 139296 | tf_op jit(solution)/shard_map/ppermute | solution.py:361
  127.5 1.8 %shard_map.91 = (bf16[2,128,2,128]{3,2,1,0:T(2,128)(2,1)}, f32[2,2]{1,0:T(2,128)}) custom-call(s32[16,16]{1,0:T(8,128)S(1)} %copy-done.1, s32[32]{0:T(128)S(1)} %copy-done.2, f32[32]{0:T(128)S(1)} %copy-done.4, s32[2,2]{1,0:T(2,128)S(1)} %copy-done.3, bf16[544,128]{1,0:T(8,128)(2,1)S(1)} %collective-permute-done.30.both_ref, f32[16,128]{1,0:T(8,128)S(1)} %bitcast.34), custom_call_target="tpu_custom_call" | custom-call | tf_op jit(solution)/shard_map/pallas_call | solution.py:238
  (86 shorter events, 12.5 us)
Async XLA Ops:
  8.0 2.2 %collective-permute-start = (bf16[1,480,512]{2,1,0:T(8,128)(2,1)}, bf16[1,480,512]{2,1,0:T(8,128)(2,1)S(1)}, u32[]{:S(2)}, u32[]{:S(2)}) collective-permute-start(bf16[1,480,512]{2,1,0:T(8,128)(2,1)} %get-tuple-element.48), channel_id=1, source_target_pairs={{0,1},{1,0},{2,3},{3,2},{4,5},{5,4},{6,7},{7,6},{8,9},{9,8},{10,11... | collective-permute-start | bytes 1474568 | tf_op jit(solution)/shard_map/ppermute | solution.py:294
  10.1 9.4 %collective-permute-start.1 = (bf16[5,480,512]{2,1,0:T(8,128)(2,1)}, bf16[5,480,512]{2,1,0:T(8,128)(2,1)S(1)}, u32[]{:S(2)}, u32[]{:S(2)}) collective-permute-start(bf16[5,480,512]{2,1,0:T(8,128)(2,1)} %get-tuple-element.49), channel_id=1, source_target_pairs={{0,1},{1,0},{2,3},{3,2},{4,5},{5,4},{6,7},{7,6},{8,9},{9,8},{10,11... | collective-permute-start | bytes 7372808 | tf_op jit(solution)/shard_map/ppermute | solution.py:294
  10.3 6.2 %collective-permute-start.2 = (bf16[2,480,512]{2,1,0:T(8,128)(2,1)}, bf16[2,480,512]{2,1,0:T(8,128)(2,1)S(1)}, u32[]{:S(2)}, u32[]{:S(2)}) collective-permute-start(bf16[2,480,512]{2,1,0:T(8,128)(2,1)} %get-tuple-element.55), channel_id=1, source_target_pairs={{0,1},{1,0},{2,3},{3,2},{4,5},{5,4},{6,7},{7,6},{8,9},{9,8},{10,11... | collective-permute-start | bytes 2949128 | tf_op jit(solution)/shard_map/ppermute | solution.py:294
  11.9 9.4 %collective-permute-start.13 = (bf16[120,512]{1,0:T(8,128)(2,1)S(1)}, bf16[120,512]{1,0:T(8,128)(2,1)S(1)}, u32[]{:S(2)}, u32[]{:S(2)}) collective-permute-start(bf16[120,512]{1,0:T(8,128)(2,1)S(1)} %get-tuple-element.77), channel_id=1, source_target_pairs={{0,14},{1,15},{2,0},{3,1},{4,2},{5,3},{6,4},{7,5},{8,6},{9,7},{10,... | collective-permute-start | bytes 368648 | tf_op jit(solution)/shard_map/ppermute | solution.py:296
  12.1 9.3 %collective-permute-start.12 = (bf16[120,512]{1,0:T(8,128)(2,1)S(1)}, bf16[120,512]{1,0:T(8,128)(2,1)S(1)}, u32[]{:S(2)}, u32[]{:S(2)}) collective-permute-start(bf16[120,512]{1,0:T(8,128)(2,1)S(1)} %get-tuple-element.75), channel_id=1, source_target_pairs={{0,2},{1,3},{2,4},{3,5},{4,6},{5,7},{6,8},{7,9},{8,10},{9,11},{10,... | collective-permute-start | bytes 368648 | tf_op jit(solution)/shard_map/ppermute | solution.py:295
  15.2 10.4 %collective-permute-start.4 = (bf16[120,512]{1,0:T(8,128)(2,1)S(1)}, bf16[120,512]{1,0:T(8,128)(2,1)S(1)}, u32[]{:S(2)}, u32[]{:S(2)}) collective-permute-start(bf16[120,512]{1,0:T(8,128)(2,1)S(1)} %get-tuple-element.61), channel_id=1, source_target_pairs={{0,14},{1,15},{2,0},{3,1},{4,2},{5,3},{6,4},{7,5},{8,6},{9,7},{10,... | collective-permute-start | bytes 368648 | tf_op jit(solution)/shard_map/ppermute | solution.py:296
  16.4 9.1 %collective-permute-start.3 = (bf16[120,512]{1,0:T(8,128)(2,1)S(1)}, bf16[120,512]{1,0:T(8,128)(2,1)S(1)}, u32[]{:S(2)}, u32[]{:S(2)}) collective-permute-start(bf16[120,512]{1,0:T(8,128)(2,1)S(1)} %get-tuple-element.59), channel_id=1, source_target_pairs={{0,2},{1,3},{2,4},{3,5},{4,6},{5,7},{6,8},{7,9},{8,10},{9,11},{10,... | collective-permute-start | bytes 368648 | tf_op jit(solution)/shard_map/ppermute | solution.py:295
  21.4 10.1 %collective-permute-start.15 = (bf16[240,512]{1,0:T(8,128)(2,1)S(1)}, bf16[240,512]{1,0:T(8,128)(2,1)S(1)}, u32[]{:S(2)}, u32[]{:S(2)}) collective-permute-start(bf16[240,512]{1,0:T(8,128)(2,1)S(1)} %pad_maximum_fusion.4), channel_id=1, source_target_pairs={{0,14},{1,15},{2,0},{3,1},{4,2},{5,3},{6,4},{7,5},{8,6},{9,7},{10,... | collective-permute-start | bytes 737288 | tf_op jit(solution)/shard_map/ppermute | solution.py:296
  22.2 9.7 %collective-permute-start.14 = (bf16[240,512]{1,0:T(8,128)(2,1)S(1)}, bf16[240,512]{1,0:T(8,128)(2,1)S(1)}, u32[]{:S(2)}, u32[]{:S(2)}) collective-permute-start(bf16[240,512]{1,0:T(8,128)(2,1)S(1)} %pad_maximum_fusion.3), channel_id=1, source_target_pairs={{0,2},{1,3},{2,4},{3,5},{4,6},{5,7},{6,8},{7,9},{8,10},{9,11},{10,... | collective-permute-start | bytes 737288 | tf_op jit(solution)/shard_map/ppermute | solution.py:295
  25.7 11.1 %collective-permute-start.6 = (bf16[240,512]{1,0:T(8,128)(2,1)S(1)}, bf16[240,512]{1,0:T(8,128)(2,1)S(1)}, u32[]{:S(2)}, u32[]{:S(2)}) collective-permute-start(bf16[240,512]{1,0:T(8,128)(2,1)S(1)} %pad_maximum_fusion.2), channel_id=1, source_target_pairs={{0,14},{1,15},{2,0},{3,1},{4,2},{5,3},{6,4},{7,5},{8,6},{9,7},{10,... | collective-permute-start | bytes 737288 | tf_op jit(solution)/shard_map/ppermute | solution.py:296
  25.8 11.4 %collective-permute-start.5 = (bf16[240,512]{1,0:T(8,128)(2,1)S(1)}, bf16[240,512]{1,0:T(8,128)(2,1)S(1)}, u32[]{:S(2)}, u32[]{:S(2)}) collective-permute-start(bf16[240,512]{1,0:T(8,128)(2,1)S(1)} %pad_maximum_fusion.1), channel_id=1, source_target_pairs={{0,2},{1,3},{2,4},{3,5},{4,6},{5,7},{6,8},{7,9},{8,10},{9,11},{10,... | collective-permute-start | bytes 737288 | tf_op jit(solution)/shard_map/ppermute | solution.py:295
  32.0 10.8 %collective-permute-start.17 = (bf16[240,512]{1,0:T(8,128)(2,1)S(1)}, bf16[240,512]{1,0:T(8,128)(2,1)S(1)}, u32[]{:S(2)}, u32[]{:S(2)}) collective-permute-start(bf16[240,512]{1,0:T(8,128)(2,1)S(1)} %add_convert_fusion.3), channel_id=1, source_target_pairs={{0,14},{1,15},{2,0},{3,1},{4,2},{5,3},{6,4},{7,5},{8,6},{9,7},{10,... | collective-permute-start | bytes 737288 | tf_op jit(solution)/shard_map/ppermute | solution.py:296
  32.6 10.2 %collective-permute-start.16 = (bf16[240,512]{1,0:T(8,128)(2,1)S(1)}, bf16[240,512]{1,0:T(8,128)(2,1)S(1)}, u32[]{:S(2)}, u32[]{:S(2)}) collective-permute-start(bf16[240,512]{1,0:T(8,128)(2,1)S(1)} %add_convert_fusion.4), channel_id=1, source_target_pairs={{0,2},{1,3},{2,4},{3,5},{4,6},{5,7},{6,8},{7,9},{8,10},{9,11},{10,... | collective-permute-start | bytes 737288 | tf_op jit(solution)/shard_map/ppermute | solution.py:295
  37.2 9.0 %collective-permute-start.8 = (bf16[240,512]{1,0:T(8,128)(2,1)S(1)}, bf16[240,512]{1,0:T(8,128)(2,1)S(1)}, u32[]{:S(2)}, u32[]{:S(2)}) collective-permute-start(bf16[240,512]{1,0:T(8,128)(2,1)S(1)} %add_convert_fusion.8), channel_id=1, source_target_pairs={{0,14},{1,15},{2,0},{3,1},{4,2},{5,3},{6,4},{7,5},{8,6},{9,7},{10,... | collective-permute-start | bytes 737288 | tf_op jit(solution)/shard_map/ppermute | solution.py:296
  37.3 10.4 %collective-permute-start.7 = (bf16[240,512]{1,0:T(8,128)(2,1)S(1)}, bf16[240,512]{1,0:T(8,128)(2,1)S(1)}, u32[]{:S(2)}, u32[]{:S(2)}) collective-permute-start(bf16[240,512]{1,0:T(8,128)(2,1)S(1)} %add_convert_fusion.9), channel_id=1, source_target_pairs={{0,2},{1,3},{2,4},{3,5},{4,6},{5,7},{6,8},{7,9},{8,10},{9,11},{10,... | collective-permute-start | bytes 737288 | tf_op jit(solution)/shard_map/ppermute | solution.py:295
  42.9 10.1 %collective-permute-start.18 = (bf16[240,512]{1,0:T(8,128)(2,1)S(1)}, bf16[240,512]{1,0:T(8,128)(2,1)S(1)}, u32[]{:S(2)}, u32[]{:S(2)}) collective-permute-start(bf16[240,512]{1,0:T(8,128)(2,1)S(1)} %add_convert_fusion.2), channel_id=1, source_target_pairs={{0,2},{1,3},{2,4},{3,5},{4,6},{5,7},{6,8},{7,9},{8,10},{9,11},{10,... | collective-permute-start | bytes 737288 | tf_op jit(solution)/shard_map/ppermute | solution.py:295
  46.3 8.6 %collective-permute-start.19 = (bf16[240,512]{1,0:T(8,128)(2,1)S(1)}, bf16[240,512]{1,0:T(8,128)(2,1)S(1)}, u32[]{:S(2)}, u32[]{:S(2)}) collective-permute-start(bf16[240,512]{1,0:T(8,128)(2,1)S(1)} %add_convert_fusion.1), channel_id=1, source_target_pairs={{0,14},{1,15},{2,0},{3,1},{4,2},{5,3},{6,4},{7,5},{8,6},{9,7},{10,... | collective-permute-start | bytes 737288 | tf_op jit(solution)/shard_map/ppermute | solution.py:296
  47.8 9.8 %collective-permute-start.10 = (bf16[240,512]{1,0:T(8,128)(2,1)S(1)}, bf16[240,512]{1,0:T(8,128)(2,1)S(1)}, u32[]{:S(2)}, u32[]{:S(2)}) collective-permute-start(bf16[240,512]{1,0:T(8,128)(2,1)S(1)} %add_convert_fusion.6), channel_id=1, source_target_pairs={{0,14},{1,15},{2,0},{3,1},{4,2},{5,3},{6,4},{7,5},{8,6},{9,7},{10,... | collective-permute-start | bytes 737288 | tf_op jit(solution)/shard_map/ppermute | solution.py:296
  49.6 8.9 %collective-permute-start.9 = (bf16[240,512]{1,0:T(8,128)(2,1)S(1)}, bf16[240,512]{1,0:T(8,128)(2,1)S(1)}, u32[]{:S(2)}, u32[]{:S(2)}) collective-permute-start(bf16[240,512]{1,0:T(8,128)(2,1)S(1)} %add_convert_fusion.7), channel_id=1, source_target_pairs={{0,2},{1,3},{2,4},{3,5},{4,6},{5,7},{6,8},{7,9},{8,10},{9,11},{10,... | collective-permute-start | bytes 737288 | tf_op jit(solution)/shard_map/ppermute | solution.py:295
  55.0 9.0 %collective-permute-start.20 = (bf16[240,512]{1,0:T(8,128)(2,1)S(1)}, bf16[240,512]{1,0:T(8,128)(2,1)S(1)}, u32[]{:S(2)}, u32[]{:S(2)}) collective-permute-start(bf16[240,512]{1,0:T(8,128)(2,1)S(1)} %add_convert_fusion), channel_id=1, source_target_pairs={{0,2},{1,3},{2,4},{3,5},{4,6},{5,7},{6,8},{7,9},{8,10},{9,11},{10,... | collective-permute-start | bytes 737288 | tf_op jit(solution)/shard_map/ppermute | solution.py:295
  56.9 8.8 %collective-permute-start.23 = (bf16[240,512]{1,0:T(8,128)(2,1)S(1)}, bf16[240,512]{1,0:T(8,128)(2,1)S(1)}, u32[]{:S(2)}, u32[]{:S(2)}) collective-permute-start(bf16[240,512]{1,0:T(8,128)(2,1)S(1)} %add_convert_fusion), channel_id=1, source_target_pairs={{0,14},{1,15},{2,0},{3,1},{4,2},{5,3},{6,4},{7,5},{8,6},{9,7},{10,... | collective-permute-start | bytes 737288 | tf_op jit(solution)/shard_map/ppermute | solution.py:296
  58.6 10.6 %collective-permute-start.11 = (bf16[240,512]{1,0:T(8,128)(2,1)S(1)}, bf16[240,512]{1,0:T(8,128)(2,1)S(1)}, u32[]{:S(2)}, u32[]{:S(2)}) collective-permute-start(bf16[240,512]{1,0:T(8,128)(2,1)S(1)} %add_convert_fusion.5), channel_id=1, source_target_pairs={{0,2},{1,3},{2,4},{3,5},{4,6},{5,7},{6,8},{7,9},{8,10},{9,11},{10,... | collective-permute-start | bytes 737288 | tf_op jit(solution)/shard_map/ppermute | solution.py:295
  62.1 7.4 %collective-permute-start.21 = (bf16[240,512]{1,0:T(8,128)(2,1)S(1)}, bf16[240,512]{1,0:T(8,128)(2,1)S(1)}, u32[]{:S(2)}, u32[]{:S(2)}) collective-permute-start(bf16[240,512]{1,0:T(8,128)(2,1)S(1)} %add_convert_fusion.5), channel_id=1, source_target_pairs={{0,14},{1,15},{2,0},{3,1},{4,2},{5,3},{6,4},{7,5},{8,6},{9,7},{10,... | collective-permute-start | bytes 737288 | tf_op jit(solution)/shard_map/ppermute | solution.py:296
  65.6 18.2 %collective-permute-start.26 = (bf16[240,512]{1,0:T(8,128)(2,1)S(1)}, bf16[240,512]{1,0:T(8,128)(2,1)S(1)}, u32[]{:S(2)}, u32[]{:S(2)}) collective-permute-start(bf16[240,512]{1,0:T(8,128)(2,1)S(1)} %collective-permute-done.20), channel_id=1, source_target_pairs={{0,2},{1,3},{2,4},{3,5},{4,6},{5,7},{6,8},{7,9},{8,10},{9,11},{10,... | collective-permute-start | bytes 737288 | tf_op jit(solution)/shard_map/ppermute | solution.py:295
  69.5 8.3 %collective-permute-start.25 = (bf16[240,512]{1,0:T(8,128)(2,1)S(1)}, bf16[240,512]{1,0:T(8,128)(2,1)S(1)}, u32[]{:S(2)}, u32[]{:S(2)}) collective-permute-start(bf16[240,512]{1,0:T(8,128)(2,1)S(1)} %collective-permute-done.11), channel_id=1, source_target_pairs={{0,2},{1,3},{2,4},{3,5},{4,6},{5,7},{6,8},{7,9},{8,10},{9,11},{10,... | collective-permute-start | bytes 737288 | tf_op jit(solution)/shard_map/ppermute | solution.py:295
  72.5 11.3 %collective-permute-start.24 = (bf16[240,512]{1,0:T(8,128)(2,1)S(1)}, bf16[240,512]{1,0:T(8,128)(2,1)S(1)}, u32[]{:S(2)}, u32[]{:S(2)}) collective-permute-start(bf16[240,512]{1,0:T(8,128)(2,1)S(1)} %collective-permute-done.23), channel_id=1, source_target_pairs={{0,14},{1,15},{2,0},{3,1},{4,2},{5,3},{6,4},{7,5},{8,6},{9,7},{10,... | collective-permute-start | bytes 737288 | tf_op jit(solution)/shard_map/ppermute | solution.py:296
  72.5 11.3 %collective-permute-start.22 = (bf16[240,512]{1,0:T(8,128)(2,1)S(1)}, bf16[240,512]{1,0:T(8,128)(2,1)S(1)}, u32[]{:S(2)}, u32[]{:S(2)}) collective-permute-start(bf16[240,512]{1,0:T(8,128)(2,1)S(1)} %collective-permute-done.21), channel_id=1, source_target_pairs={{0,14},{1,15},{2,0},{3,1},{4,2},{5,3},{6,4},{7,5},{8,6},{9,7},{10,... | collective-permute-start | bytes 737288 | tf_op jit(solution)/shard_map/ppermute | solution.py:296
  73.5 11.0 %collective-permute-start.27 = (bf16[10,272,128]{2,1,0:T(8,128)(2,1)S(1)}, bf16[10,272,128]{2,1,0:T(8,128)(2,1)S(1)}, u32[]{:S(2)}, u32[]{:S(2)}) collective-permute-start(bf16[10,272,128]{2,1,0:T(8,128)(2,1)S(1)} %shard_map.87), channel_id=1, source_target_pairs={{0,1},{1,0},{2,3},{3,2},{4,5},{5,4},{6,7},{7,6},{8,9},{9,8},{10,11... | collective-permute-start | bytes 2088968 | tf_op jit(solution)/shard_map/ppermute | solution.py:294
  84.4 1.8 %collective-permute-start.28 = (bf16[6,272,128]{2,1,0:T(8,128)(2,1)S(1)}, bf16[6,272,128]{2,1,0:T(8,128)(2,1)S(1)}, u32[]{:S(2)}, u32[]{:S(2)}) collective-permute-start(bf16[6,272,128]{2,1,0:T(8,128)(2,1)S(1)} %shard_map.89), channel_id=1, source_target_pairs={{0,1},{1,0},{2,3},{3,2},{4,5},{5,4},{6,7},{7,6},{8,9},{9,8},{10,11... | collective-permute-start | bytes 1253384 | tf_op jit(solution)/shard_map/ppermute | solution.py:294
  86.9 40.6 %copy-start = (f32[2048]{0:T(1024)S(1)}, f32[2048]{0:T(1024)}, u32[]{:S(2)}) copy-start(f32[2048]{0:T(1024)} %param.11) | copy-start | bytes 24580
  112.3 1.3 %collective-permute-start.29 = (bf16[272,128]{1,0:T(8,128)(2,1)S(1)}, bf16[272,128]{1,0:T(8,128)(2,1)S(1)}, u32[]{:S(2)}, u32[]{:S(2)}) collective-permute-start(bf16[272,128]{1,0:T(8,128)(2,1)S(1)} %reduce_sum.12), channel_id=1, source_target_pairs={{0,1},{1,0},{2,3},{3,2},{4,5},{5,4},{6,7},{7,6},{8,9},{9,8},{10,11... | collective-permute-start | bytes 208904 | tf_op jit(solution)/shard_map/ppermute | solution.py:294
  113.6 13.9 %collective-permute-start.30 = (bf16[544,128]{1,0:T(8,128)(2,1)S(1)}, bf16[544,128]{1,0:T(8,128)(2,1)S(1)}, u32[]{:S(2)}, u32[]{:S(2)}) collective-permute-start(bf16[544,128]{1,0:T(8,128)(2,1)S(1)} %pad_maximum_fusion.5), channel_id=1, source_target_pairs={{0,2},{1,32},{16,3},{17,48},{32,18},{33,33},{48,19},{49,49},{64,22... | collective-permute-start | bytes 417800 | tf_op jit(solution)/shard_map/ppermute | solution.py:361
  (5 other events, 173.8 us)
